TPU v7x, 128 devices: a whole 4x4x4 slice. The times are simulated.
128 devices in a mesh: dp: 16 (over x, y), tensor: 8 (over z, core).
Axes of the slice: x: 4, y: 4, z: 4, core: 2. Of those that a mesh axis runs over, the one named last changes fastest.
Arguments:
- residual: bfloat16 [128, 7168], P(('dp', 'tensor')), may hold values from -6 to 6
- query_latent: bfloat16 [128, 64, 576], P(('dp', 'tensor')), may hold values from -16 to 16
- latent_cache: bfloat16 [128, 4096, 576], P(('dp', 'tensor')), may hold values from -5 to 5
- lengths: int32 [128], P(('dp', 'tensor')), may hold values from 2 to 4096
- w_uv: bfloat16 [64, 512, 128], P('tensor'), may hold values from -0.25 to 0.25
- w_o: bfloat16 [64, 128, 7168], P('tensor', 'dp'), may hold values from -1.75 to 1.75
- norm_gain: float32 [7168], replicated, may hold values from 0.1 to 1.9
- expert_ids: int32 [128, 8], P(('dp', 'tensor')), may hold values from 0 to 15, all different within a row; in each aligned block of 8 rows (0 to 7, 8 to 15, ...) at most 5 rows name the same one
- route_weights: float32 [128, 8], P(('dp', 'tensor')), may hold values from 0.1 to 0.6
- w_gate: bfloat16 [16, 7168, 2048], P('dp', None, 'tensor'), may hold values from -0.0625 to 0.0625
- w_up: bfloat16 [16, 7168, 2048], P('dp', None, 'tensor'), may hold values from -0.0625 to 0.0625
- w_down: bfloat16 [16, 2048, 7168], P('dp', 'tensor'), may hold values from -0.125 to 0.125
Outputs:
- layer_output: bfloat16 [128, 7168], P(('dp', 'tensor'))
Inputs may be any that keep to these rules, and one draw needn't show every extreme that they name: `expert_ids`: each row names 8 different experts. Within the rows of one index of dp (aligned blocks of 8 rows) no expert is named by more than 5 rows, a bound that some block reaches.
All inputs are finite; a program needn't handle non-finite values.
Results may differ from a plain program's by a relative error of at most 0.0085.
Values may be sent and summed in bfloat16 or wider, within the bound.
A program may use at most 64 MiB of HBM per device.

v0:
```python
import jax
import jax.numpy as jnp
from jax import lax
from jax.sharding import PartitionSpec as P

masked_score = -1e30
norm_eps = 1e-06


def expert_apply(slots, w_gate, w_up, w_down):
    gate_val = jnp.einsum("slrd,ldf->slrf", slots, w_gate, preferred_element_type=jnp.float32)
    up_val = jnp.einsum("slrd,ldf->slrf", slots, w_up, preferred_element_type=jnp.float32)
    activation = (jax.nn.silu(gate_val) * up_val).astype(jnp.bfloat16)
    return jnp.einsum("slrf,lfd->slrd", activation, w_down, preferred_element_type=jnp.float32)


def on_device(
    residual,
    query_latent,
    latent_cache,
    lengths,
    w_uv,
    w_o,
    norm_gain,
    expert_ids,
    route_weights,
    w_gate,
    w_up,
    w_down,
):
    n_tensor = lax.axis_size("tensor")
    n_data = lax.axis_size("dp")
    my_rows = residual.shape[0]
    width_all = query_latent.shape[2]
    latent_width = w_uv.shape[1]
    head_dim = w_uv.shape[2]
    score_scale = (head_dim + width_all - latent_width) ** (-0.5)
    slot_index = lax.iota(jnp.int32, latent_cache.shape[1])
    active = (slot_index[None, :] < lengths[:, None])[:, None, :]
    scores = (
        jnp.einsum("rhc,rpc->rhp", query_latent, latent_cache, preferred_element_type=jnp.float32)
        * score_scale
    )
    scores = jnp.where(active, scores, masked_score)
    row_max = jnp.max(scores, axis=2, keepdims=True)
    weights = jnp.where(active, jnp.exp(scores - row_max), 0.0)
    totals = jnp.sum(weights, axis=2)
    summed = jnp.einsum(
        "rhp,rpc->rhc",
        weights.astype(jnp.bfloat16),
        latent_cache[:, :, :latent_width],
        preferred_element_type=jnp.float32,
    )
    latent = (summed / totals[:, :, None]).astype(jnp.bfloat16)
    own_heads = lax.all_to_all(latent, "tensor", split_axis=1, concat_axis=0, tiled=True)
    values = jnp.einsum("rhc,hcv->rhv", own_heads, w_uv, preferred_element_type=jnp.float32).astype(
        jnp.bfloat16
    )
    spread = lax.all_to_all(values, "dp", split_axis=2, concat_axis=0, tiled=True)
    projected = jnp.einsum("rhv,hvn->rn", spread, w_o, preferred_element_type=jnp.float32)
    summed_all = lax.psum(projected, ("dp", "tensor"))
    owner_index = lax.axis_index("dp") * n_tensor + lax.axis_index("tensor")
    attended = lax.dynamic_slice_in_dim(summed_all, owner_index * my_rows, my_rows, 0)
    stream = residual.astype(jnp.float32) + attended
    normed = (
        stream * lax.rsqrt(jnp.mean(stream * stream, axis=1, keepdims=True) + norm_eps) * norm_gain
    ).astype(jnp.bfloat16)
    local_experts = w_gate.shape[0]
    expert_total = local_experts * n_data
    model_width = residual.shape[1]
    chosen = expert_ids[:, :, None] == lax.iota(jnp.int32, expert_total)[None, None, :]
    coefficient = jnp.sum(jnp.where(chosen, route_weights[:, :, None], 0.0), axis=1)
    routed = jnp.any(chosen, axis=1)
    outgoing = jnp.where(
        routed.T[:, :, None], normed[None, :, :], jnp.zeros_like(normed)[None, :, :]
    )
    outgoing = outgoing.reshape(n_data, local_experts, my_rows, model_width)
    widened = jnp.broadcast_to(
        outgoing[:, None], (n_data, n_tensor, local_experts, my_rows, model_width)
    )
    widened = widened.reshape(n_data * n_tensor, local_experts, my_rows, model_width)
    arrived = lax.all_to_all(widened, ("dp", "tensor"), split_axis=0, concat_axis=0, tiled=True)
    produced = expert_apply(arrived, w_gate, w_up, w_down)
    returned = lax.all_to_all(
        produced.astype(jnp.bfloat16), ("dp", "tensor"), split_axis=0, concat_axis=0, tiled=True
    ).astype(produced.dtype)
    results = jnp.sum(
        returned.reshape(n_data, n_tensor, local_experts, my_rows, model_width), axis=1
    )
    results = results.reshape(expert_total, my_rows, model_width)
    mixture = jnp.sum(coefficient.T[:, :, None] * results, axis=0)
    return (stream + mixture).astype(jnp.bfloat16)


def solution(mesh):
    return jax.shard_map(
        on_device,
        mesh=mesh,
        in_specs=(
            P(("dp", "tensor"), None),
            P(("dp", "tensor"), None, None),
            P(("dp", "tensor"), None, None),
            P(("dp", "tensor")),
            P("tensor", None, None),
            P("tensor", "dp", None),
            P(),
            P(("dp", "tensor"), None),
            P(("dp", "tensor"), None),
            P("dp", None, "tensor"),
            P("dp", None, "tensor"),
            P("dp", "tensor", None),
        ),
        out_specs=P(("dp", "tensor"), None),
        check_vma=False,
    )
```

profile of v0, /device:TPU:0, one launch (start us, length us, event | category | flops | bytes accessed | tf_op | source)
XLA Modules:
  0.0 317.9 jit_solution(1677639125107247591)
XLA Ops:
  6.5 0.0 copy-start
  6.5 0.0 all-reduce.2.cloned.1.call-start
  6.5 0.0 copy-start.1
  7.4 3.8 %fusion.78 = (f32[64]{0:T(128)S(1)}, f32[64,4096]{1,0:T(8,128)S(1)}) fusion(bf16[1,4096,576]{1,2,0:T(8,128)(2,1)} %param.14, bf16[1,64,576]{2,1,0:T(8,128)(2,1)} %param.13, pred[4096]{0:T(1024)(128)(4,1)S(1)} %iota_compare_fusion), kind=kOutput, calls=%fused_computation.59 | convolution fusion | flops 302776256 | bytes 5845248 | tf_op jit(solution)/shard_map/rhc,rpc->rhp/dot_general | solution.py:41
  11.1 0.4 fusion.54
  11.5 0.0 copy-done.1
  11.5 0.0 copy-start.2
  11.5 1.4 fusion.51
  12.9 0.1 copy.58
  13.0 0.5 broadcast.148
  13.5 1.0 reduce.11
  14.6 10.8 %all_to_all.40 = bf16[8,2,2048]{2,1,0:T(2,128)(2,1)S(1)} all-to-all(bf16[8,2,2048]{2,1,0:T(2,128)(2,1)S(1)} %reshape.268), channel_id=1, replica_groups=mesh['dp'=16,'tensor'=8] {'tensor'}, dimensions={0} | all-to-all | bytes 131072 | tf_op jit(solution)/shard_map/all_to_all | solution.py:55
  25.4 0.1 reshape.269
  25.5 0.0 copy-done
  25.5 0.2 fusion.44
  25.8 0.2 copy.32
  26.0 0.3 reshape.270
  26.2 14.4 %all_to_all.41 = bf16[16,2,256]{2,1,0:T(2,128)(2,1)S(1)} all-to-all(bf16[16,2,256]{2,1,0:T(2,128)(2,1)S(1)} %reshape.270), channel_id=1, replica_groups=mesh['dp'=16,'tensor'=8] {'dp'}, dimensions={0} | all-to-all | bytes 32768 | tf_op jit(solution)/shard_map/all_to_all | solution.py:59
  40.7 0.3 reshape.271
  41.0 0.2 copy.34
  41.2 0.2 all_to_all.33
  41.4 0.0 copy-done.2
  41.4 0.0 copy-start.5
  41.4 0.0 copy-start.4
  41.5 0.0 copy-start.3
  41.5 2.5 convolution_bitcast_fusion
  44.0 0.0 all-reduce.2.cloned.1.call-update
  44.0 0.0 copy-done.5
  44.0 0.1 fusion.75
  44.1 149.0 %all-reduce.2.cloned.1.call-done = f32[128,7168]{1,0:T(8,128)} async-done(((f32[128,7168]{1,0:T(8,128)}), f32[128,7168]{1,0:T(8,128)}) %all-reduce.2.cloned.1.call-update) | async-done | bytes 3670032 | tf_op jit(solution)/shard_map/psum | solution.py:61
  193.1 0.0 copy-done.4
  193.1 1.6 multiply_reduce_fusion
  195.4 0.0 copy-done.3
  195.4 0.1 convert_reduce_fusion
  195.5 0.1 broadcast_select_fusion
  195.5 0.2 broadcast_bitcast_fusion
  195.8 2.7 reduce.12
  198.5 4.6 %reshape.272 = bf16[128,2,3584]{2,1,0:T(2,128)(2,1)S(1)} reshape(bf16[128,7168]{1,0:T(8,128)(2,1)} %reduce.12) | data formatting | bytes 3670016
  203.1 34.5 %all_to_all.42 = bf16[128,2,3584]{2,1,0:T(2,128)(2,1)} all-to-all(bf16[128,2,3584]{2,1,0:T(2,128)(2,1)S(1)} %reshape.272), channel_id=1, replica_groups=mesh['dp'=16,'tensor'=8] {'dp','tensor'}, dimensions={0} | all-to-all | bytes 3670016 | tf_op jit(solution)/shard_map/all_to_all | solution.py:82
  237.6 11.5 %reshape.273 = bf16[128,1,1,7168]{3,2,1,0:T(2,128)(2,1)} reshape(bf16[128,2,3584]{2,1,0:T(2,128)(2,1)} %all_to_all.42) | data formatting | bytes 3670016
  249.1 3.9 %fusion.19 = f32[128,1,1,256]{3,0,2,1:T(8,128)S(1)} fusion(bf16[1,7168,256]{2,1,0:T(8,128)(2,1)} %param.21, bf16[128,1,1,7168]{3,2,1,0:T(2,128)(2,1)} %reshape.273), kind=kOutput, calls=%fused_computation.18 | convolution fusion | flops 469762048 | bytes 5636096 | tf_op jit(solution)/shard_map/slrd,ldf->slrf/dot_general | solution.py:11
  253.0 7.6 %fusion = bf16[128,1,1,7168]{3,0,2,1:T(8,128)(2,1)} fusion(bf16[1,256,7168]{2,1,0:T(8,128)(2,1)} %param.23, bf16[1,7168,256]{2,1,0:T(8,128)(2,1)} %param.22, bf16[128,1,1,7168]{3,2,1,0:T(2,128)(2,1)} %reshape.273, f32[128,1,1,256]{3,0,2,1:T(8,128)S(1)} %fusion.19), kind=kOutput, calls=%fused_computation.2 | convolution fusion | flops 940638208 | bytes 11141120 | tf_op jit(solution)/shard_map/slrf,lfd->slrd/dot_general | solution.py:14
  260.6 3.6 %reduce.13 = bf16[128,7168]{1,0:T(8,128)(2,1)S(1)} reduce(bf16[128,1,1,7168]{3,0,2,1:T(8,128)(2,1)} %fusion, bf16[]{:T(256)} %broadcast.148), dimensions={1,2}, to_apply=%copy.36.reduce_sub_computation | reduce | bytes 3670018 | tf_op jit(solution)/shard_map/convert_element_type | solution.py:85
  264.2 0.0 copy-start.6
  264.2 2.3 reshape.274
  266.6 4.6 %all-to-all-start.3 = ((bf16[128,2,3584]{2,1,0:T(2,128)(2,1)}), bf16[128,2,3584]{2,1,0:T(2,128)(2,1)S(1)}, u32[]{:S(2)}, u32[]{:S(2)}) async-start(bf16[128,2,3584]{2,1,0:T(2,128)(2,1)} %reshape.274), calls=%async_computation.3 | async-start | bytes 3670016 | tf_op jit(solution)/shard_map/all_to_all | solution.py:84
  271.2 0.0 copy-done.6
  271.2 0.1 select_reduce_fusion
  271.3 27.7 %all-to-all-done.3 = bf16[128,2,3584]{2,1,0:T(2,128)(2,1)S(1)} async-done(((bf16[128,2,3584]{2,1,0:T(2,128)(2,1)}), bf16[128,2,3584]{2,1,0:T(2,128)(2,1)S(1)}, u32[]{:S(2)}, u32[]{:S(2)}) %all-to-all-start.3) | async-done | bytes 1835040 | tf_op jit(solution)/shard_map/all_to_all | solution.py:84
  299.0 4.0 %reshape.275 = bf16[128,1,1,7168]{3,2,1,0:T(2,128)(2,1)} reshape(bf16[128,2,3584]{2,1,0:T(2,128)(2,1)S(1)} %all-to-all-done.3) | data formatting | bytes 3670016
  303.0 5.8 %reshape.264 = f32[128,1,1,7168]{3,2,1,0:T(1,128)S(1)} convert(bf16[128,1,1,7168]{3,2,1,0:T(2,128)(2,1)} %reshape.275) | non-fusion elementwise | flops 917504 | bytes 5505024 | tf_op jit(solution)/shard_map/reshape | solution.py:88
  308.8 1.5 bitcast_reduce_fusion
  310.3 0.1 fusion.66
  310.4 0.6 add_convert_fusion
  (3 shorter events, 0.1 us)
Async XLA Ops:
  6.5 19.0 %copy-start = (bf16[8,512,128]{2,1,0:T(8,128)(2,1)S(1)}, bf16[8,512,128]{2,1,0:T(8,128)(2,1)}, u32[]{:S(2)}) copy-start(bf16[8,512,128]{2,1,0:T(8,128)(2,1)} %param.16) | copy-start | bytes 3145732
  6.5 186.6 %all-reduce.2.cloned.1.call-start = ((), (), s32[]{:S(2)}) async-start(), calls=%async_computation.4 | async-start | bytes 7340032 | tf_op jit(solution)/shard_map/psum | solution.py:61
  6.5 5.0 %copy-start.1 = (bf16[1,4096,576]{1,2,0:T(8,128)(2,1)S(1)}, bf16[1,4096,576]{1,2,0:T(8,128)(2,1)}, u32[]{:S(2)}) copy-start(bf16[1,4096,576]{1,2,0:T(8,128)(2,1)} %param.14) | copy-start | bytes 14155780
  11.5 29.9 %copy-start.2 = (bf16[8,8,7168]{2,1,0:T(8,128)(2,1)S(1)}, bf16[8,8,7168]{2,1,0:T(8,128)(2,1)}, u32[]{:S(2)}) copy-start(bf16[8,8,7168]{2,1,0:T(8,128)(2,1)} %param.17) | copy-start | bytes 2752516
  41.4 2.6 copy-start.5
  41.4 151.7 %copy-start.4 = (bf16[1,7168]{1,0:T(2,128)(2,1)S(1)}, bf16[1,7168]{1,0:T(2,128)(2,1)}, u32[]{:S(2)}) copy-start(bf16[1,7168]{1,0:T(2,128)(2,1)} %param.12) | copy-start | bytes 43012
  41.5 153.9 %copy-start.3 = (f32[7168]{0:T(1024)S(1)}, f32[7168]{0:T(1024)}, u32[]{:S(2)}) copy-start(f32[7168]{0:T(1024)} %param.18) | copy-start | bytes 86020
  264.2 7.0 %copy-start.6 = (f32[1,8]{1,0:T(1,128)S(1)}, f32[1,8]{1,0:T(1,128)}, u32[]{:S(2)}) copy-start(f32[1,8]{1,0:T(1,128)} %param.20) | copy-start | bytes 100
  266.6 32.5 %all-to-all-start.3 = ((bf16[128,2,3584]{2,1,0:T(2,128)(2,1)}), bf16[128,2,3584]{2,1,0:T(2,128)(2,1)S(1)}, u32[]{:S(2)}, u32[]{:S(2)}) async-start(bf16[128,2,3584]{2,1,0:T(2,128)(2,1)} %reshape.274), calls=%async_computation.3 | async-start | bytes 3670016 | tf_op jit(solution)/shard_map/all_to_all | solution.py:84
Sparse Core Ops, SparseCore 0:
  44.1 148.9 all-reduce.1
where the time goes:
time: 319 us; the launch traced here: 318 us
  waiting for transfers between devices  177 us (55%)
  blocking collectives  59.8 us (19%)
  local copies, waits for them, and re-layouts  24.6 us (8%)
  matrix products  19.5 us (6%)
  other arithmetic  17.7 us (6%)
  between operations  15 us (5%)
  starting transfers between devices  4.65 us (1%)
    psum x1, waiting for transfers between devices, on_device(): summed_all = lax.psum(projected, ('dp', 'tensor'))  149 us
    all_to_all x1, blocking collectives, on_device(): lax.all_to_all(widened, ('dp', 'tensor'), split_axis=0, concat_axis=0, ti...  34.5 us
    all_to_all x1, waiting for transfers between devices, on_device(): lax.all_to_all(produced.astype(jnp.bfloat16), ('dp', 'tensor'), split_axi...  27.7 us
    unnamed x24, local copies, waits for them, and re-layouts  23.6 us
    all_to_all x1, blocking collectives, on_device(): lax.all_to_all(values, 'dp', split_axis=2, concat_axis=0, tiled=True)  14.4 us
    all_to_all x1, blocking collectives, on_device(): lax.all_to_all(latent, 'tensor', split_axis=1, concat_axis=0, tiled=True)  10.8 us
    dot_general x1, matrix products, expert_apply(): jnp.einsum('slrf,lfd->slrd', activation, w_down, preferred_element_type=j...  7.59 us
  transfers between devices with their start and end apart: 2, of which 2 were waited for; matrix products, arithmetic and copies ran while one was open for 0% of the time, Pallas kernels for 0%

commit v1 on v0

v1 whole, which is shorter than its diff:
```python
import jax
import jax.numpy as jnp
from jax import lax
from jax.experimental import pallas as pl
from jax.experimental.pallas import tpu as pltpu
from jax.sharding import PartitionSpec as P

MESH = pl.DeviceIdType.MESH
F32 = jnp.float32
BF16 = jnp.bfloat16

CTX, CW, LAT = 4096, 576, 512
D, H, HD, FF = 7168, 64, 128, 256
CHUNK = 512
NCHUNK = CTX // CHUNK
WIN = 512
SCALE = 192 ** (-0.5)
EPS = 1e-06
MASKED = -1e30
PARTS = ((0, 2304), (2304, 2304), (4608, 2560))
ORDERS = (("z", "y", "x"), ("x", "z", "y"), ("y", "x", "z"))
TILE_ORDER = (0, 1, 2, 0)
SPAN = 24


def window_start(dp):
    return (dp // 2) * 896 + (dp % 2) * 384


def onehot(n, source):
    row = lax.broadcasted_iota(jnp.int32, (n, n), 0)
    col = lax.broadcasted_iota(jnp.int32, (n, n), 1)
    return jnp.where(col == source(row), 1.0, 0.0).astype(BF16)


def dot(a, b):
    return jnp.dot(a, b, preferred_element_type=F32)


def layer(
    len_ref, ids_ref, rw_ref, res_ref, q_ref, gain_ref,
    cache_hbm, wuv_hbm, wo_hbm, wg_hbm, wu_hbm, wd_hbm,
    out_ref,
    cache_v, wuv_v, wg_v, wu_v, wd_v,
    s_ref, resb_v, wo_recv, lat_send, lat_recv, vals_send, vals_all,
    rs_send, rs_recv, st_send, st_recv, x_v, ig2_v,
    d_own, c_send, c_recv, p1, p1r, q2f, q2, q2r, q3, q3r, mix_v,
    local_sem, a2a_s, a2a_r, rb_s, rb_r, lat_s, lat_r, val_s, val_r,
    rs_s, rs_r, st_s, st_r, ag_s, ag_r, sib_s, sib_r,
    cs_s, cs_r, p1_s, p1_r, p2_s, p2_r, p3_s, p3_r,
):
    dp = lax.axis_index("dp")
    t = lax.axis_index("tensor")
    pos = {"x": dp // 4, "y": dp % 4, "z": t // 2, "c": t % 2}
    core = pos["c"]

    def at_dp(i):
        return {"dp": lax.rem(dp + i, 16), "tensor": t}

    def at_t(i):
        return {"dp": dp, "tensor": lax.rem(t + i, 8)}

    def along(axis, i):
        new = dict(pos)
        new[axis] = lax.rem(pos[axis] + i, 4)
        return {"dp": new["x"] * 4 + new["y"], "tensor": new["z"] * 2 + new["c"]}

    sibling = {"dp": dp, "tensor": pos["z"] * 2 + (1 - core)}

    def remote(src, dst, ss, rs, dev):
        return pltpu.make_async_remote_copy(
            src_ref=src, dst_ref=dst, send_sem=ss, recv_sem=rs, device_id=dev, device_id_type=MESH
        )

    def each(n, f):
        def step(i, carry):
            f(i)
            return carry

        lax.fori_loop(1, n, step, 0)

    barrier = pltpu.get_barrier_semaphore()
    each(16, lambda i: pl.semaphore_signal(barrier, inc=1, device_id=at_dp(i), device_id_type=MESH))
    each(8, lambda i: pl.semaphore_signal(barrier, inc=1, device_id=at_t(i), device_id_type=MESH))

    def cache_copy(i):
        return pltpu.make_async_copy(
            cache_hbm.at[0, pl.ds(pl.multiple_of(i * CHUNK, CHUNK), CHUNK)],
            cache_v.at[i],
            local_sem.at[i],
        )

    def start_cache(i, carry):
        cache_copy(i).start()
        return carry

    lax.fori_loop(0, NCHUNK, start_cache, 0)

    start = pl.multiple_of(window_start(dp), 128)
    resb_v[...] = jnp.broadcast_to(res_ref[...].astype(F32), (8, D)).astype(BF16)
    own_wo = pltpu.make_async_copy(
        wo_hbm.at[:, :, pl.ds(start, WIN)], wo_recv.at[pl.ds(0, 8), dp], local_sem.at[NCHUNK]
    )
    own_wo.start()
    wo_recv[8, dp] = resb_v[:, pl.ds(start, WIN)]
    gain = gain_ref[...]
    ig2_v[...] = 1.0 / (gain * gain)

    pl.semaphore_wait(barrier, 22)

    def wo_copy(i):
        there = lax.rem(dp + i, 16)
        first = pl.multiple_of(window_start(there), 128)
        return remote(
            wo_hbm.at[:, :, pl.ds(first, WIN)], wo_recv.at[pl.ds(0, 8), dp],
            a2a_s.at[i], a2a_r.at[i], at_dp(i),
        )

    def res_copy(i):
        there = lax.rem(dp + i, 16)
        first = pl.multiple_of(window_start(there), 128)
        return remote(
            resb_v.at[:, pl.ds(first, WIN)], wo_recv.at[8, dp], rb_s.at[i], rb_r.at[i], at_dp(i)
        )

    each(16, lambda i: wo_copy(i).start())
    each(16, lambda i: res_copy(i).start())
    wuv_copy = pltpu.make_async_copy(wuv_hbm, wuv_v, local_sem.at[NCHUNK + 1])
    wuv_copy.start()

    length = len_ref[0]
    q = q_ref[0]

    def score(i, top):
        cache_copy(i).wait()
        s = lax.dot_general(
            q, cache_v[i], (((1,), (1,)), ((), ())), preferred_element_type=F32
        ) * SCALE
        slot = lax.broadcasted_iota(jnp.int32, (H, CHUNK), 1) + i * CHUNK
        s = jnp.where(slot < length, s, MASKED)
        s_ref[i] = s
        return jnp.maximum(top, jnp.max(s, axis=1, keepdims=True))

    top = lax.fori_loop(0, NCHUNK, score, jnp.full((H, 1), MASKED, F32))

    w_copies = [
        pltpu.make_async_copy(src, dst, local_sem.at[NCHUNK + 2 + k])
        for k, (src, dst) in enumerate(((wg_hbm, wg_v), (wu_hbm, wu_v), (wd_hbm, wd_v)))
    ]
    for copy in w_copies:
        copy.start()

    def mix(i, carry):
        total, acc = carry
        slot = lax.broadcasted_iota(jnp.int32, (H, CHUNK), 1) + i * CHUNK
        w = jnp.where(slot < length, jnp.exp(s_ref[i] - top), 0.0)
        total = total + jnp.sum(w, axis=1, keepdims=True)
        return total, acc + dot(w.astype(BF16), cache_v[i, :, :LAT])

    total, acc = lax.fori_loop(
        0, NCHUNK, mix, (jnp.zeros((H, 1), F32), jnp.zeros((H, LAT), F32))
    )
    latent = acc / total

    lane = lax.broadcasted_iota(jnp.int32, (1, 128), 1)
    coef = jnp.zeros((1, 128), F32)
    for k in range(8):
        coef = jnp.where(jnp.bitwise_and(lane, 15) == ids_ref[0, k], rw_ref[0, k], coef)
    high = coef.astype(BF16).astype(F32)
    coef = jnp.where(lane < 16, high, jnp.where(lane < 32, coef - high, 0.0))

    lat_send[:, :, :LAT] = latent.reshape(8, 8, LAT).astype(BF16)
    lat_send[:, :, LAT:] = jnp.broadcast_to(coef.reshape(1, 1, 128), (8, 8, 128)).astype(BF16)
    lat_recv[t] = lat_send[t]

    def lat_copy(i):
        return remote(
            lat_send.at[lax.rem(t + i, 8)], lat_recv.at[t], lat_s.at[i], lat_r.at[i], at_t(i)
        )

    def lat_wait(i):
        src = lax.rem(t - i + 8, 8)
        remote(lat_send.at[src], lat_recv.at[src], lat_s.at[i], lat_r.at[i], at_t(i)).wait_recv()

    each(8, lambda i: lat_copy(i).start())
    wuv_copy.wait()
    each(8, lat_wait)

    by_head = onehot(64, lambda r: jnp.bitwise_and(r, 7) * 8 + jnp.right_shift(r, 3))
    lat = lat_recv[...].astype(F32).reshape(64, LAT + 128).astype(BF16)
    lat = dot(by_head, lat)
    pieces = [dot(lat[8 * h : 8 * h + 8, :LAT].astype(BF16), wuv_v[h]) for h in range(8)]
    pieces.append(lat[0:8, LAT:])
    vals_send[...] = jnp.concatenate(pieces, axis=1).astype(BF16)
    vals_all[dp] = vals_send[...]

    def val_copy(i):
        return remote(vals_send, vals_all.at[dp], val_s.at[i], val_r.at[i], at_dp(i))

    def val_wait(i):
        src = lax.rem(dp - i + 16, 16)
        remote(vals_send, vals_all.at[src], val_s.at[i], val_r.at[i], at_dp(i)).wait_recv()

    each(16, lambda i: val_copy(i).start())

    def wo_wait(i):
        src = lax.rem(dp - i + 16, 16)
        remote(
            wo_hbm.at[:, :, pl.ds(start, WIN)], wo_recv.at[pl.ds(0, 8), src],
            a2a_s.at[i], a2a_r.at[i], at_dp(i),
        ).wait_recv()
        remote(
            resb_v.at[:, pl.ds(start, WIN)], wo_recv.at[8, src], rb_s.at[i], rb_r.at[i], at_dp(i)
        ).wait_recv()

    own_wo.wait()
    each(16, wo_wait)
    each(16, val_wait)

    to_t_order = onehot(128, lambda r: jnp.bitwise_and(r, 15) * 8 + jnp.right_shift(r, 4))
    vals = vals_all[...].astype(F32).reshape(128, 1152).astype(BF16)
    vals = dot(to_t_order, vals)
    row = lax.broadcasted_iota(jnp.int32, (128, 128), 0)
    col = lax.broadcasted_iota(jnp.int32, (128, 128), 1)
    pick = jnp.where(
        (jnp.right_shift(row, 4) == t) & (col == jnp.bitwise_and(row, 15) * 8), 1.0, 0.0
    ).astype(BF16)
    part = dot(pick, wo_recv[8].astype(F32).reshape(128, WIN).astype(BF16))
    for h in range(8):
        part = part + dot(
            vals[:, h * HD : (h + 1) * HD].astype(BF16),
            wo_recv[h].astype(F32).reshape(128, WIN).astype(BF16),
        )
    rs_send[...] = part.astype(BF16).reshape(8, 16, WIN)
    coefs = vals[:, 1024:]
    mine = (col == dp) | (col == dp + 16)
    coef_col = jnp.sum(jnp.where(mine, coefs, 0.0), axis=1, keepdims=True)

    def rs_copy(i):
        return remote(
            rs_send.at[lax.rem(t + i, 8)], rs_recv.at[t], rs_s.at[i], rs_r.at[i], at_t(i)
        )

    def rs_wait(i):
        src = lax.rem(t - i + 8, 8)
        remote(rs_send.at[src], rs_recv.at[src], rs_s.at[i], rs_r.at[i], at_t(i)).wait_recv()

    each(8, lambda i: rs_copy(i).start())
    rs_recv[t] = rs_send[t]
    each(8, rs_wait)
    stream = rs_recv[0].astype(F32)
    for k in range(1, 8):
        stream = stream + rs_recv[k].astype(F32)
    scaled = (stream * gain_ref[:, pl.ds(start, WIN)]).astype(BF16)
    for j in range(4):
        x_v[j, pos["x"], pos["y"], pos["z"], core] = scaled[:, 128 * j : 128 * j + 128]

    def block(j, free, fixed):
        at = dict(pos)
        at.update(fixed)
        index = [pl.ds(0, 4) if a in free else at[a] for a in ("x", "y", "z")]
        return x_v.at[j, index[0], index[1], index[2], at["c"]]

    def gather(j, phase, i):
        order = ORDERS[TILE_ORDER[j]]
        here = block(j, order[:phase], {})
        n = (j * 3 + phase) * 3 + i - 1
        return remote(here, here, ag_s.at[n], ag_r.at[n], along(order[phase], i))

    def gather_wait(j, phase, i):
        order = ORDERS[TILE_ORDER[j]]
        axis = order[phase]
        there = block(j, order[:phase], {axis: lax.rem(pos[axis] - i + 4, 4)})
        n = (j * 3 + phase) * 3 + i - 1
        remote(there, there, ag_s.at[n], ag_r.at[n], along(axis, i)).wait_recv()

    def to_sibling(j, i, c):
        order = ORDERS[TILE_ORDER[j]]
        axis = order[2]
        there = block(j, order[:2], {axis: lax.rem(pos[axis] - i + 4, 4), "c": c})
        return remote(there, there, sib_s.at[j * 4 + i], sib_r.at[j * 4 + i], sibling)

    for phase in range(3):
        for j in range(4):
            if phase:
                for i in (1, 2, 3):
                    gather_wait(j, phase - 1, i)
            for i in (2, 1, 3):
                gather(j, phase, i).start()
            if phase == 2:
                to_sibling(j, 0, core).start()

    st_send[...] = jnp.zeros_like(st_send)
    for j in range(4):
        st_send[pl.ds(j, 16, stride=8), :] = stream[:, 128 * j : 128 * j + 128]
    st_recv[dp] = st_send[pl.ds(pl.multiple_of(dp * 8, 8), 8), :]

    def st_copy(i):
        there = pl.multiple_of(lax.rem(dp + i, 16) * 8, 8)
        return remote(
            st_send.at[pl.ds(there, 8)], st_recv.at[dp], st_s.at[i], st_r.at[i], at_dp(i)
        )

    def st_wait(i):
        src = lax.rem(dp - i + 16, 16)
        remote(
            st_send.at[pl.ds(0, 8)], st_recv.at[src], st_s.at[i], st_r.at[i], at_dp(i)
        ).wait_recv()

    each(16, lambda i: st_copy(i).start())

    for i in (1, 3, 2):
        for j in range(4):
            gather_wait(j, 2, i)
            to_sibling(j, i, core).start()
    for i in (0, 1, 3, 2):
        for j in range(4):
            to_sibling(j, i, 1 - core).wait_recv()
    for copy in w_copies:
        copy.wait()

    def up_step(k, carry):
        g, u, sq = carry
        tiles = []
        for odd in range(2):
            for j in range(odd, 4):
                tiles.append(x_v[j, k // 2, 2 * lax.rem(k, 2) + odd].reshape(128, 128))
        for n, tile in enumerate(tiles):
            f = tile.astype(F32)
            sq = sq + f * f * ig2_v[:, pl.ds(pl.multiple_of(k * 896 + n * 128, 128), 128)]
        x = jnp.concatenate(tiles, axis=1)
        rows = pl.ds(pl.multiple_of(k * 896, 896), 896)
        return g + dot(x, wg_v[rows, :]), u + dot(x, wu_v[rows, :]), sq

    zero = jnp.zeros((128, FF), F32)
    g, u, sq = lax.fori_loop(0, 8, up_step, (zero, zero, jnp.zeros((128, 128), F32)))
    factor = lax.rsqrt(jnp.sum(sq, axis=1, keepdims=True) * (1.0 / D) + EPS)
    g = g * factor
    act = (g / (1.0 + jnp.exp(-g))) * (u * factor * coef_col)
    act = act.astype(BF16)

    bits = {"z": (5, 3), "c": (4, 1), "x": (2, 3), "y": (0, 3)}

    def core_copy(p):
        w = PARTS[p][1]
        return remote(
            c_send.at[p, :, pl.ds(0, w)], c_recv.at[p, :, pl.ds(0, w)], cs_s.at[p], cs_r.at[p], sibling
        )

    for p, (first, w) in enumerate(PARTS):
        order = ORDERS[p]

        def source(r):
            src = jnp.left_shift(jnp.bitwise_xor(jnp.right_shift(r, 6), core), 4)
            for a, shift in zip(order, (4, 2, 0)):
                src = src + jnp.left_shift(
                    jnp.bitwise_and(jnp.right_shift(r, shift), 3), bits[a][0]
                )
            return src

        act_p = dot(onehot(128, source), act).astype(BF16)

        def down(n, carry):
            o = dot(act_p, wd_v[:, pl.ds(pl.multiple_of(first + n * 256, 256), 256)])
            cols = pl.ds(pl.multiple_of(n * 256, 256), 256)
            d_own[p, :, cols] = o[:64]
            c_send[p, :, cols] = o[64:].astype(BF16)
            return carry

        lax.fori_loop(0, w // 256, down, 0)
        core_copy(p).start()

    def sum1(p, i):
        w = PARTS[p][1]
        axis = ORDERS[p][0]
        n = p * 3 + i - 1
        return remote(
            p1.at[p, lax.rem(pos[axis] + i, 4), :, pl.ds(0, w)], p1r.at[p, i - 1, :, pl.ds(0, w)],
            p1_s.at[n], p1_r.at[n], along(axis, i),
        )

    for p, (first, w) in enumerate(PARTS):
        core_copy(p).wait_recv()

        def pair(n, carry):
            cols = pl.ds(pl.multiple_of(n * 256, 256), 256)
            o = d_own[p, :, cols] + c_recv[p, :, cols].astype(F32)
            p1[p, :, :, cols] = o.reshape(4, 16, 256).astype(BF16)
            return carry

        lax.fori_loop(0, w // 256, pair, 0)
        for i in (2, 1, 3):
            sum1(p, i).start()

    def sum2(p, i):
        axis = ORDERS[p][1]
        n = p * 3 + i - 1
        return remote(
            q2.at[p, lax.rem(pos[axis] + i, 4)], q2r.at[p, i - 1], p2_s.at[n], p2_r.at[n], along(axis, i)
        )

    q2f[...] = jnp.zeros_like(q2f)
    for p, (first, w) in enumerate(PARTS):
        for i in (1, 3, 2):
            sum1(p, i).wait_recv()
        o = p1[p, pos[ORDERS[p][0]], :, 0:w].astype(F32)
        for i in range(3):
            o = o + p1r[p, i, :, 0:w].astype(F32)
        for j in range(w // 128):
            q2f[pl.ds(j, 16, stride=SPAN), :] = o[:, 128 * j : 128 * j + 128]
        q2[p] = q2f[...].astype(BF16).reshape(4, 4 * SPAN, 128)
        for i in (2, 1, 3):
            sum2(p, i).start()

    def sum3(p, i):
        axis = ORDERS[p][2]
        n = p * 3 + i - 1
        return remote(
            q3.at[p, lax.rem(pos[axis] + i, 4)], q3r.at[p, i - 1], p3_s.at[n], p3_r.at[n], along(axis, i)
        )

    for p in range(3):
        for i in (1, 3, 2):
            sum2(p, i).wait_recv()
        o = q2[p, pos[ORDERS[p][1]]].astype(F32)
        for i in range(3):
            o = o + q2r[p, i].astype(F32)
        q3[p] = o.reshape(4, SPAN, 128)
        for i in (2, 1, 3):
            sum3(p, i).start()

    each(16, st_wait)
    for k in range(8):
        mix_v[7 * k : 7 * k + 4, :] = st_recv[2 * k, 0:4, :]
        mix_v[7 * k + 4 : 7 * k + 7, :] = st_recv[2 * k + 1, 1:4, :]

    for p, (first, w) in enumerate(PARTS):
        for i in (1, 3, 2):
            sum3(p, i).wait_recv()
        o = q3[p, pos[ORDERS[p][2]]]
        for i in range(3):
            o = o + q3r[p, i]
        tiles = slice(first // 128, (first + w) // 128)
        mix_v[tiles, :] = mix_v[tiles, :] + o[: w // 128]
    out_ref[...] = mix_v[...].astype(BF16)

    each(16, lambda i: wo_copy(i).wait_send())
    each(16, lambda i: res_copy(i).wait_send())
    each(8, lambda i: lat_copy(i).wait_send())
    each(16, lambda i: val_copy(i).wait_send())
    each(8, lambda i: rs_copy(i).wait_send())
    each(16, lambda i: st_copy(i).wait_send())
    for j in range(4):
        for phase in range(3):
            for i in (1, 2, 3):
                gather(j, phase, i).wait_send()
        for i in range(4):
            to_sibling(j, i, core).wait_send()
    for p in range(3):
        core_copy(p).wait_send()
        for i in (1, 2, 3):
            sum1(p, i).wait_send()
            sum2(p, i).wait_send()
            sum3(p, i).wait_send()


def on_device(
    residual, query_latent, latent_cache, lengths, w_uv, w_o, norm_gain, expert_ids, route_weights,
    w_gate, w_up, w_down,
):
    dma = pltpu.SemaphoreType.DMA
    vmem = pl.BlockSpec(memory_space=pltpu.VMEM)
    smem = pl.BlockSpec(memory_space=pltpu.SMEM)
    hbm = pl.BlockSpec(memory_space=pl.ANY)
    wide = max(w for _, w in PARTS)
    out = pl.pallas_call(
        layer,
        out_shape=jax.ShapeDtypeStruct((D // 128, 128), BF16),
        in_specs=[smem, smem, smem, vmem, vmem, vmem] + [hbm] * 6,
        out_specs=vmem,
        scratch_shapes=[
            pltpu.VMEM((NCHUNK, CHUNK, CW), BF16),
            pltpu.VMEM((8, LAT, HD), BF16),
            pltpu.VMEM((D, FF), BF16),
            pltpu.VMEM((D, FF), BF16),
            pltpu.VMEM((FF, D), BF16),
            pltpu.VMEM((NCHUNK, H, CHUNK), F32),
            pltpu.VMEM((8, D), BF16),
            pltpu.VMEM((9, 16, 8, WIN), BF16),
            pltpu.VMEM((8, 8, LAT + 128), BF16),
            pltpu.VMEM((8, 8, LAT + 128), BF16),
            pltpu.VMEM((8, 1152), BF16),
            pltpu.VMEM((16, 8, 1152), BF16),
            pltpu.VMEM((8, 16, WIN), BF16),
            pltpu.VMEM((8, 16, WIN), BF16),
            pltpu.VMEM((128, 128), F32),
            pltpu.VMEM((16, 8, 128), F32),
            pltpu.VMEM((4, 4, 4, 4, 2, 16, 128), BF16),
            pltpu.VMEM((1, D), F32),
            pltpu.VMEM((3, 64, wide), F32),
            pltpu.VMEM((3, 64, wide), BF16),
            pltpu.VMEM((3, 64, wide), BF16),
            pltpu.VMEM((3, 4, 16, wide), BF16),
            pltpu.VMEM((3, 3, 16, wide), BF16),
            pltpu.VMEM((16 * SPAN, 128), F32),
            pltpu.VMEM((3, 4, 4 * SPAN, 128), BF16),
            pltpu.VMEM((3, 3, 4 * SPAN, 128), BF16),
            pltpu.VMEM((3, 4, SPAN, 128), F32),
            pltpu.VMEM((3, 3, SPAN, 128), F32),
            pltpu.VMEM((D // 128, 128), F32),
            dma((NCHUNK + 5,)),
            dma((16,)), dma((16,)), dma((16,)), dma((16,)),
            dma((8,)), dma((8,)), dma((16,)), dma((16,)),
            dma((8,)), dma((8,)), dma((16,)), dma((16,)),
            dma((36,)), dma((36,)), dma((16,)), dma((16,)),
            dma((3,)), dma((3,)), dma((9,)), dma((9,)), dma((9,)), dma((9,)), dma((9,)), dma((9,)),
        ],
        compiler_params=pltpu.CompilerParams(
            collective_id=0, has_side_effects=True, vmem_limit_bytes=56 * 1024 * 1024
        ),
    )(
        lengths, expert_ids, route_weights, residual, query_latent, norm_gain.reshape(1, D),
        latent_cache, w_uv, w_o, w_gate.reshape(D, FF), w_up.reshape(D, FF), w_down.reshape(FF, D),
    )
    return out.reshape(1, D)


def solution(mesh):
    return jax.shard_map(
        on_device,
        mesh=mesh,
        in_specs=(
            P(("dp", "tensor"), None),
            P(("dp", "tensor"), None, None),
            P(("dp", "tensor"), None, None),
            P(("dp", "tensor")),
            P("tensor", None, None),
            P("tensor", "dp", None),
            P(),
            P(("dp", "tensor"), None),
            P(("dp", "tensor"), None),
            P("dp", None, "tensor"),
            P("dp", None, "tensor"),
            P("dp", "tensor", None),
        ),
        out_specs=P(("dp", "tensor"), None),
        check_vma=False,
    )
```

time: 319 us -> 86.8 us (0.27)
  waiting for transfers between devices: 177 us -> 0 us
  Pallas kernels: 0 us -> 76.8 us
  blocking collectives: 59.8 us -> 0 us
  matrix products: 19.5 us -> 0 us
  other arithmetic: 17.7 us -> 0 us
  local copies, waits for them, and re-layouts: 24.6 us -> 9 us
  between operations: 15 us -> 0.66 us
  starting transfers between devices: 4.65 us -> 0 us
    psum x1 -> x0, waiting for transfers between devices: 149 us -> none  [on_device(): summed_all = lax.psum(projected, ('dp', 'tensor'))]
    pallas_call x0 -> x1, Pallas kernels: none -> 76.8 us  [on_device(): pl.pallas_call(layer, out_shape=jax.ShapeDtypeStruct((D // 128, 128), BF1...]
    all_to_all x3 -> x0, blocking collectives: 59.8 us -> none  [the longest x1 34.5 us: on_device(): lax.all_to_all(widened, ('dp', 'tensor'), split_axis=0, concat_axis=0, ti...]
    all_to_all x1 -> x0, waiting for transfers between devices: 27.7 us -> none  [on_device(): lax.all_to_all(produced.astype(jnp.bfloat16), ('dp', 'tensor'), split_axi...]
    dot_general x6 -> x0, matrix products: 19.5 us -> none  [the longest x1 7.59 us: expert_apply(): jnp.einsum('slrf,lfd->slrd', activation, w_down, preferred_element_type=j...]
    unnamed x24 -> x2, local copies, waits for them, and re-layouts: 23.6 us -> 9 us
    reshape x1 -> x0, other arithmetic: 5.81 us -> none  [on_device(): returned.reshape(n_data, n_tensor, local_experts, my_rows, model_width)]
    all_to_all x1 -> x0, starting transfers between devices: 4.64 us -> none  [on_device(): lax.all_to_all(produced.astype(jnp.bfloat16), ('dp', 'tensor'), split_axi...]
  transfers between devices with their start and end apart: 2 -> 0, of which waited for: 2 -> 0; matrix products, arithmetic and copies ran while one was open for 0% -> 0% of each run, Pallas kernels for 0% -> 0%
where the time goes in v1:
time: 86.8 us; the launch traced here: 86.4 us
  Pallas kernels  76.8 us (88%)
  local copies, waits for them, and re-layouts  9 us (10%)
    pallas_call x1, Pallas kernels, on_device(): pl.pallas_call(layer, out_shape=jax.ShapeDtypeStruct((D // 128, 128), BF1...  76.8 us
    unnamed x2, local copies, waits for them, and re-layouts  9 us

profile of v1, /device:TPU:0, one launch (start us, length us, event | category | flops | bytes accessed | tf_op | source)
XLA Modules:
  0.0 86.4 jit_solution(622829808711908236)
XLA Ops:
  0.7 7.7 %copy.13.cache_hbm = bf16[1,4096,576]{2,1,0:T(8,128)(2,1)} copy(bf16[1,4096,576]{1,2,0:T(8,128)(2,1)} %param.14) | data formatting | bytes 9437184 | tf_op args[2]
  8.3 76.8 %shard_map.118 = bf16[56,128]{1,0:T(8,128)(2,1)} custom-call(s32[1]{0:T(128)S(6)} %copy.17.len_ref, s32[1,8]{1,0:T(1,128)} %ids_ref.1, f32[1,8]{1,0:T(1,128)} %rw_ref.1, bf16[1,7168]{1,0:T(2,128)(2,1)} %res_ref.1, bf16[1,64,576]{2,1,0:T(8,128)(2,1)} %q_ref.1, f32[1,7168]{1,0:T(1,128)} %bitcast.13, bf16[1,4096,576]{2,1,0:T(8,128)(2,1)} %copy.13.cache_hbm, ...), custom_call_target="tpu_custom_call" | custom-call | tf_op jit(solution)/shard_map/pallas_call | solution.py:476
  85.1 1.3 %copy.16 = bf16[1,1,56,128]{3,1,2,0:T(2,128)(2,1)} copy(bf16[1,1,56,128]{3,2,1,0:T(8,128)(2,1)} %bitcast.12) | data formatting | bytes 28672

commit v2 on v1

v2 whole, which is shorter than its diff:
```python
import jax
import jax.numpy as jnp
from jax import lax
from jax.experimental import pallas as pl
from jax.experimental.pallas import tpu as pltpu
from jax.sharding import PartitionSpec as P

MESH = pl.DeviceIdType.MESH
F32 = jnp.float32
BF16 = jnp.bfloat16

CTX, CW, LAT = 4096, 576, 512
D, H, HD, FF = 7168, 64, 128, 256
CHUNK = 1024
NCHUNK = CTX // CHUNK
WIN = 512
SCALE = 192 ** (-0.5)
EPS = 1e-06
MASKED = -1e30
PARTS = ((0, 2304), (2304, 2304), (4608, 2560))
PIECES = (
    (0, 0, 1280), (1, 0, 1280), (2, 0, 1280), (0, 1280, 1024), (1, 1280, 1024), (2, 1280, 1280),
)
ORDERS = (("z", "y", "x"), ("x", "z", "y"), ("y", "x", "z"))
TILE_ORDER = ((0, 1, 2, 0), (1, 2, 0, 1))
SPAN = 24
PLANE = (
    (2, 2), (2, 1), (1, 2), (2, 3), (3, 2), (2, 0), (0, 2), (1, 1), (3, 3), (1, 3), (3, 1),
    (1, 0), (0, 1), (3, 0), (0, 3),
)
LINE = ((2, 1), (2, 0), (1, 1), (3, 1), (1, 0), (3, 0), (0, 1))


def window_start(dp):
    return (dp // 2) * 896 + (dp % 2) * 384


def onehot(n, source):
    row = lax.broadcasted_iota(jnp.int32, (n, n), 0)
    col = lax.broadcasted_iota(jnp.int32, (n, n), 1)
    return jnp.where(col == source(row), 1.0, 0.0).astype(BF16)


def dot(a, b):
    return jnp.dot(a, b, preferred_element_type=F32)


def layer(
    len_hbm, ids_hbm, rw_hbm, res_hbm, q_hbm, gain_hbm,
    cache_hbm, wuv_hbm, wo_hbm, wg_hbm, wu_hbm, wd_hbm,
    out_ref,
    len_ref, ids_ref, rw_ref, res_ref, q_ref, gain_ref,
    cache_v, wuv_v, wg_v, wu_v, wd_v,
    s_ref, resf_v, res_recv, wo_recv, lat_send, lat_recv, vals_send, vals_all,
    rs_send, rs_recv, st_send, st_recv, x_v, ig2_v,
    d_own, c_send, c_recv, p1, p1r, q2f, q2, q2r, q3, q3r, mix_v,
    local_sem, a2a_s, a2a_r, rb_s, rb_r, lat_s, lat_r, val_s, val_r,
    rs_s, rs_r, st_s, st_r, ag_s, ag_r, sib_s, sib_r,
    cs_s, cs_r, p1_s, p1_r, p2_s, p2_r, p3_s, p3_r,
):
    dp = lax.axis_index("dp")
    t = lax.axis_index("tensor")
    pos = {"x": dp // 4, "y": dp % 4, "z": t // 2, "c": t % 2}
    core = pos["c"]

    def dp_of(step):
        return lax.rem(pos["x"] + step[0], 4) * 4 + lax.rem(pos["y"] + step[1], 4)

    def dp_before(step):
        return lax.rem(pos["x"] + 4 - step[0], 4) * 4 + lax.rem(pos["y"] + 4 - step[1], 4)

    def t_of(step):
        return lax.rem(pos["z"] + step[0], 4) * 2 + lax.rem(core + step[1], 2)

    def t_before(step):
        return lax.rem(pos["z"] + 4 - step[0], 4) * 2 + lax.rem(core + step[1], 2)

    def at_dp(step):
        return {"dp": dp_of(step), "tensor": t}

    def at_t(step):
        return {"dp": dp, "tensor": t_of(step)}

    def along(axis, i):
        new = dict(pos)
        new[axis] = lax.rem(pos[axis] + i, 4)
        return {"dp": new["x"] * 4 + new["y"], "tensor": new["z"] * 2 + new["c"]}

    sibling = {"dp": dp, "tensor": pos["z"] * 2 + (1 - core)}

    def remote(src, dst, ss, rs, dev):
        return pltpu.make_async_remote_copy(
            src_ref=src, dst_ref=dst, send_sem=ss, recv_sem=rs, device_id=dev, device_id_type=MESH
        )

    def each(n, f):
        def step(i, carry):
            f(i)
            return carry

        lax.fori_loop(0, n, step, 0)

    barrier = pltpu.get_barrier_semaphore()
    for step in PLANE:
        pl.semaphore_signal(barrier, inc=1, device_id=at_dp(step), device_id_type=MESH)
    for step in LINE:
        pl.semaphore_signal(barrier, inc=1, device_id=at_t(step), device_id_type=MESH)

    def cache_copy(i):
        return pltpu.make_async_copy(
            cache_hbm.at[0, :, pl.ds(pl.multiple_of(i * CHUNK, CHUNK), CHUNK)],
            cache_v.at[i],
            local_sem.at[i],
        )

    def local(n, src, dst):
        return pltpu.make_async_copy(src, dst, local_sem.at[NCHUNK + n])

    small = [
        local(0, q_hbm.at[0], q_ref), local(1, len_hbm, len_ref), local(2, res_hbm, res_ref),
        local(3, gain_hbm, gain_ref), local(4, ids_hbm, ids_ref), local(5, rw_hbm, rw_ref),
    ]
    small[0].start()
    small[1].start()
    cache_copy(0).start()
    small[2].start()
    for i in range(1, NCHUNK):
        cache_copy(i).start()
    for copy in small[3:]:
        copy.start()
    start = pl.multiple_of(window_start(dp), 128)
    own_wo = local(6, wo_hbm.at[:, :, pl.ds(start, WIN)], wo_recv.at[:, dp])
    own_wo.start()
    wuv_copy = local(7, wuv_hbm, wuv_v)
    wuv_copy.start()

    for copy in small[:2]:
        copy.wait()
    length = len_ref[0]
    q = q_ref[...]

    def score(i, top):
        cache_copy(i).wait()
        s = dot(q, cache_v[i]) * SCALE
        slot = lax.broadcasted_iota(jnp.int32, (H, CHUNK), 1) + i * CHUNK
        s = jnp.where(slot < length, s, MASKED)
        s_ref[i] = s
        return jnp.maximum(top, jnp.max(s, axis=1, keepdims=True))

    top = jnp.full((H, 1), MASKED, F32)
    for i in range(NCHUNK // 2):
        top = score(i, top)

    small[2].wait()
    resf_v[...] = res_ref[...].astype(F32)
    pl.semaphore_wait(barrier, 22)

    def wo_copy(n, src_dp, slot, skip):
        first = pl.multiple_of(window_start(src_dp) + skip, 128)
        return remote(
            wo_hbm.at[:, :, pl.ds(first, WIN - skip)],
            wo_recv.at[:, slot, :, pl.ds(skip, WIN - skip)],
            a2a_s.at[n], a2a_r.at[n], at_dp(PLANE[n]),
        )

    def by_parity(odd, f):
        pl.when(odd == 0)(lambda: f(0))
        pl.when(odd == 1)(lambda: f(128))

    def res_copy(n):
        first = pl.multiple_of(window_start(dp_of(PLANE[n])), 128)
        return remote(
            resf_v.at[:, pl.ds(first, WIN)], res_recv.at[dp],
            rb_s.at[n], rb_r.at[n], at_dp(PLANE[n]),
        )

    for n, step in enumerate(PLANE):
        by_parity(
            lax.rem(dp_of(step), 2),
            lambda skip, n=n, step=step: wo_copy(n, dp_of(step), dp, skip).start(),
        )
    res_recv[dp] = resf_v[:, pl.ds(start, WIN)]
    for n in range(15):
        res_copy(n).start()

    for i in range(NCHUNK // 2, NCHUNK):
        top = score(i, top)

    w_copies = [local(8 + k, src, dst) for k, (src, dst) in enumerate(
        ((wg_hbm, wg_v), (wu_hbm, wu_v), (wd_hbm, wd_v)))]
    for copy in w_copies:
        copy.start()

    total = jnp.zeros((H, 1), F32)
    acc = jnp.zeros((H, LAT), F32)
    for i in range(NCHUNK):
        slot = lax.broadcasted_iota(jnp.int32, (H, CHUNK), 1) + i * CHUNK
        w = jnp.where(slot < length, jnp.exp(s_ref[i] - top), 0.0)
        total = total + jnp.sum(w, axis=1, keepdims=True)
        acc = acc + lax.dot_general(
            w.astype(BF16), cache_v[i, :LAT], (((1,), (1,)), ((), ())), preferred_element_type=F32
        )
    latent = acc / total

    for copy in small[4:]:
        copy.wait()
    lane = lax.broadcasted_iota(jnp.int32, (1, 128), 1)
    coef = jnp.zeros((1, 128), F32)
    for k in range(8):
        coef = jnp.where(jnp.bitwise_and(lane, 15) == ids_ref[0, k], rw_ref[0, k], coef)
    high = coef.astype(BF16).astype(F32)
    coef = jnp.where(lane < 16, high, jnp.where(lane < 32, coef - high, 0.0))

    lat_send[:, :, :LAT] = latent.reshape(8, 8, LAT).astype(BF16)
    lat_send[:, :, LAT:] = jnp.broadcast_to(coef.reshape(1, 1, 128), (8, 8, 128)).astype(BF16)

    def lat_copy(n):
        return remote(
            lat_send.at[t_of(LINE[n])], lat_recv.at[t], lat_s.at[n], lat_r.at[n], at_t(LINE[n])
        )

    def lat_wait(n):
        src = t_before(LINE[n])
        remote(lat_send.at[src], lat_recv.at[src], lat_s.at[n], lat_r.at[n], at_t(LINE[n])).wait_recv()

    for n in range(7):
        lat_copy(n).start()
    lat_recv[t] = lat_send[t]
    small[3].wait()
    gain = gain_ref[...]
    ig2_v[...] = 1.0 / (gain * gain)
    wuv_copy.wait()
    for n in range(7):
        lat_wait(n)

    by_head = onehot(64, lambda r: jnp.bitwise_and(r, 7) * 8 + jnp.right_shift(r, 3))
    lat = lat_recv[...].astype(F32).reshape(64, LAT + 128).astype(BF16)
    lat = dot(by_head, lat)
    pieces = [dot(lat[8 * h : 8 * h + 8, :LAT].astype(BF16), wuv_v[h]) for h in range(8)]
    pieces.append(lat[0:8, LAT:])
    vals_send[...] = jnp.concatenate(pieces, axis=1).astype(BF16)

    def val_copy(n):
        return remote(vals_send, vals_all.at[dp], val_s.at[n], val_r.at[n], at_dp(PLANE[n]))

    def val_wait(n):
        src = dp_before(PLANE[n])
        remote(vals_send, vals_all.at[src], val_s.at[n], val_r.at[n], at_dp(PLANE[n])).wait_recv()

    for n in range(15):
        val_copy(n).start()
    vals_all[dp] = vals_send[...]
    own_wo.wait()
    for n in range(15):
        by_parity(
            lax.rem(dp, 2),
            lambda skip, n=n: wo_copy(n, dp, dp_before(PLANE[n]), skip).wait_recv(),
        )
    for n in range(15):
        val_wait(n)

    to_t_order = onehot(128, lambda r: jnp.bitwise_and(r, 15) * 8 + jnp.right_shift(r, 4))
    vals_raw = vals_all[...].astype(F32).reshape(128, 1152).astype(BF16)
    vals = dot(to_t_order, vals_raw[:, : 8 * HD]).astype(BF16)
    part = jnp.zeros((128, WIN), F32)
    for h in range(8):
        part = part + dot(
            vals[:, h * HD : (h + 1) * HD], wo_recv[h].astype(F32).reshape(128, WIN).astype(BF16)
        )
    rs_send[...] = part.astype(BF16).reshape(8, 16, WIN)

    def rs_copy(n):
        return remote(
            rs_send.at[t_of(LINE[n])], rs_recv.at[t], rs_s.at[n], rs_r.at[n], at_t(LINE[n])
        )

    def rs_wait(n):
        src = t_before(LINE[n])
        remote(rs_send.at[src], rs_recv.at[src], rs_s.at[n], rs_r.at[n], at_t(LINE[n])).wait_recv()

    for n in range(7):
        rs_copy(n).start()
    rs_recv[t] = rs_send[t]

    to_c_order = onehot(
        128,
        lambda r: jnp.bitwise_and(r, 15) * 8
        + jnp.bitwise_and(jnp.right_shift(r, 4), 3) * 2
        + jnp.right_shift(r, 6),
    )
    coefs = dot(to_c_order, vals_raw[:, 8 * HD :])
    col = lax.broadcasted_iota(jnp.int32, (128, 128), 1)
    mine = (col == dp) | (col == dp + 16)
    coef_col = jnp.sum(jnp.where(mine, coefs, 0.0), axis=1, keepdims=True)

    for n in range(15):
        src = dp_before(PLANE[n])
        remote(
            resf_v.at[:, pl.ds(start, WIN)], res_recv.at[src],
            rb_s.at[n], rb_r.at[n], at_dp(PLANE[n]),
        ).wait_recv()
    res = jnp.concatenate([res_recv[k] for k in range(16)], axis=0)

    for n in range(7):
        rs_wait(n)
    stream = res
    for k in range(8):
        stream = stream + rs_recv[k].astype(F32)
    scaled = (stream * gain_ref[:, pl.ds(start, WIN)]).astype(BF16)

    def either(c, f):
        zero, one = f(0), f(1)
        return zero + c * (one - zero)

    def axis_of(j, c, k):
        return ORDERS[TILE_ORDER[c][j]][k]

    def place(j, k, c):
        return either(c, lambda v: pos[axis_of(j, v, k)])

    def block(j, phase, c, i):
        at = [place(j, k, c) for k in (2, 1, 0)][: 3 - phase]
        at[-1] = lax.rem(at[-1] - i + 4, 4)
        return x_v.at[(j, c, *at)]

    def partner(j, k, i):
        return {
            name: either(core, lambda v, name=name: along(axis_of(j, v, k), i)[name])
            for name in ("dp", "tensor")
        }

    def gather(j, phase, i):
        here = block(j, phase, core, 0)
        n = (j * 3 + phase) * 3 + i - 1
        return remote(here, here, ag_s.at[n], ag_r.at[n], partner(j, phase, i))

    def gather_wait(j, phase, i):
        there = block(j, phase, core, i)
        n = (j * 3 + phase) * 3 + i - 1
        remote(there, there, ag_s.at[n], ag_r.at[n], partner(j, phase, i)).wait_recv()

    def to_sibling(j, i, c):
        there = block(j, 2, c, i)
        return remote(there, there, sib_s.at[j * 4 + i], sib_r.at[j * 4 + i], sibling)

    for j in range(4):
        x_v[j, core, place(j, 2, core), place(j, 1, core), place(j, 0, core)] = scaled[
            :, 128 * j : 128 * j + 128
        ]
        for i in (2, 1, 3):
            gather(j, 0, i).start()

    st_send[...] = jnp.zeros_like(st_send)
    for j in range(4):
        st_send[pl.ds(j, 16, stride=8), :] = stream[:, 128 * j : 128 * j + 128]
    st_recv[dp] = st_send[pl.ds(pl.multiple_of(dp * 8, 8), 8), :]

    def st_copy(n):
        there = pl.multiple_of(dp_of(PLANE[n]) * 8, 8)
        return remote(
            st_send.at[pl.ds(there, 8)], st_recv.at[dp], st_s.at[n], st_r.at[n], at_dp(PLANE[n])
        )

    def st_wait(n):
        src = dp_before(PLANE[n])
        remote(
            st_send.at[pl.ds(0, 8)], st_recv.at[src], st_s.at[n], st_r.at[n], at_dp(PLANE[n])
        ).wait_recv()

    for phase in (1, 2):
        for j in range(4):
            for i in (1, 3, 2):
                gather_wait(j, phase - 1, i)
            for i in (2, 1, 3):
                gather(j, phase, i).start()
            if phase == 2:
                to_sibling(j, 0, core).start()

    for n in range(15):
        st_copy(n).start()
    for n in range(15):
        by_parity(
            lax.rem(dp_of(PLANE[n]), 2),
            lambda skip, n=n: wo_copy(n, dp_of(PLANE[n]), dp, skip).wait_send(),
        )
        res_copy(n).wait_send()
        val_copy(n).wait_send()
    for n in range(7):
        lat_copy(n).wait_send()
        rs_copy(n).wait_send()

    for i in (1, 3, 2):
        for j in range(4):
            gather_wait(j, 2, i)
            to_sibling(j, i, core).start()
    for i in (0, 1, 3, 2):
        for j in range(4):
            to_sibling(j, i, 1 - core).wait_recv()
    for copy in w_copies:
        copy.wait()

    def tile_of(j, x, y):
        halves = []
        for c in range(2):
            at = {"x": x, "y": y, "z": slice(None)}
            i1, i2, i3 = (at[a] for a in ORDERS[TILE_ORDER[c][j]])
            halves.append(x_v[j, c, i3, i2, i1].reshape(64, 128))
        return jnp.concatenate(halves, axis=0)

    def up_step(k, carry):
        g, u, sq = carry
        tiles = []
        for odd in range(2):
            for j in range(odd, 4):
                tiles.append(tile_of(j, k // 2, 2 * lax.rem(k, 2) + odd))
        for n, tile in enumerate(tiles):
            f = tile.astype(F32)
            sq = sq + f * f * ig2_v[:, pl.ds(pl.multiple_of(k * 896 + n * 128, 128), 128)]
        x = jnp.concatenate(tiles, axis=1)
        rows = pl.ds(pl.multiple_of(k * 896, 896), 896)
        return g + dot(x, wg_v[rows, :]), u + dot(x, wu_v[rows, :]), sq

    zero = jnp.zeros((128, FF), F32)
    g, u, sq = lax.fori_loop(0, 8, up_step, (zero, zero, jnp.zeros((128, 128), F32)))
    factor = lax.rsqrt(jnp.sum(sq, axis=1, keepdims=True) * (1.0 / D) + EPS)
    g = g * factor
    act = (g / (1.0 + jnp.exp(-g))) * (u * factor * coef_col)
    act = act.astype(BF16)

    bits = {"c": 6, "z": 4, "x": 2, "y": 0}
    acts = []
    for p in range(3):

        def source(r):
            src = jnp.left_shift(jnp.bitwise_xor(jnp.right_shift(r, 6), core), bits["c"])
            for a, shift in zip(ORDERS[p], (4, 2, 0)):
                src = src + jnp.left_shift(jnp.bitwise_and(jnp.right_shift(r, shift), 3), bits[a])
            return src

        acts.append(dot(onehot(128, source), act).astype(BF16))

    def core_copy(s):
        p, at, w = PIECES[s]
        cols = pl.ds(at, w)
        return remote(
            c_send.at[p, :, cols], c_recv.at[p, :, cols], cs_s.at[s], cs_r.at[s], sibling
        )

    def sum1(s, i):
        p, at, w = PIECES[s]
        axis = ORDERS[p][0]
        n = s * 3 + i - 1
        cols = pl.ds(at, w)
        return remote(
            p1.at[p, lax.rem(pos[axis] + i, 4), :, cols], p1r.at[p, i - 1, :, cols],
            p1_s.at[n], p1_r.at[n], along(axis, i),
        )

    def down(s):
        p, at, w = PIECES[s]
        first = PARTS[p][0] + at
        o = dot(acts[p], wd_v[:, first : first + w])
        d_own[p, :, at : at + w] = o[:64]
        c_send[p, :, at : at + w] = o[64:].astype(BF16)
        core_copy(s).start()

    def pair(s):
        p, at, w = PIECES[s]
        core_copy(s).wait_recv()
        o = d_own[p, :, at : at + w] + c_recv[p, :, at : at + w].astype(F32)
        p1[p, :, :, at : at + w] = o.reshape(4, 16, w).astype(BF16)
        for i in (2, 1, 3):
            sum1(s, i).start()

    down(0)
    for s in range(1, 6):
        down(s)
        pair(s - 1)
    pair(5)

    def sum2(p, i):
        axis = ORDERS[p][1]
        n = p * 3 + i - 1
        return remote(
            q2.at[p, lax.rem(pos[axis] + i, 4)], q2r.at[p, i - 1], p2_s.at[n], p2_r.at[n], along(axis, i)
        )

    q2f[...] = jnp.zeros_like(q2f)
    for p, (first, w) in enumerate(PARTS):
        for s in (p, p + 3):
            for i in (1, 3, 2):
                sum1(s, i).wait_recv()
        o = p1[p, pos[ORDERS[p][0]], :, 0:w].astype(F32)
        for i in range(3):
            o = o + p1r[p, i, :, 0:w].astype(F32)
        for j in range(w // 128):
            q2f[pl.ds(j, 16, stride=SPAN), :] = o[:, 128 * j : 128 * j + 128]
        q2[p] = q2f[...].astype(BF16).reshape(4, 4 * SPAN, 128)
        for i in (2, 1, 3):
            sum2(p, i).start()

    def sum3(p, i):
        axis = ORDERS[p][2]
        n = p * 3 + i - 1
        return remote(
            q3.at[p, lax.rem(pos[axis] + i, 4)], q3r.at[p, i - 1], p3_s.at[n], p3_r.at[n], along(axis, i)
        )

    for n in range(15):
        st_wait(n)
        st_copy(n).wait_send()
    for k in range(8):
        mix_v[7 * k : 7 * k + 4, :] = st_recv[2 * k, 0:4, :]
        mix_v[7 * k + 4 : 7 * k + 7, :] = st_recv[2 * k + 1, 1:4, :]

    for p in range(3):
        for i in (1, 3, 2):
            sum2(p, i).wait_recv()
        o = q2[p, pos[ORDERS[p][1]]].astype(F32)
        for i in range(3):
            o = o + q2r[p, i].astype(F32)
        q3[p] = o.reshape(4, SPAN, 128)
        for i in (2, 1, 3):
            sum3(p, i).start()

    for j in range(4):
        for phase in range(3):
            for i in (1, 2, 3):
                gather(j, phase, i).wait_send()
        for i in range(4):
            to_sibling(j, i, core).wait_send()
    for s in range(6):
        core_copy(s).wait_send()
        for i in (1, 2, 3):
            sum1(s, i).wait_send()
    for p in range(3):
        for i in (1, 2, 3):
            sum2(p, i).wait_send()

    for p, (first, w) in enumerate(PARTS):
        for i in (1, 3, 2):
            sum3(p, i).wait_recv()
        o = q3[p, pos[ORDERS[p][2]]]
        for i in range(3):
            o = o + q3r[p, i]
        tiles = slice(first // 128, (first + w) // 128)
        mix_v[tiles, :] = mix_v[tiles, :] + o[: w // 128]
    out_ref[...] = mix_v[...].astype(BF16)
    for p in range(3):
        for i in (1, 2, 3):
            sum3(p, i).wait_send()


def on_device(
    residual, query_latent, latent_cache, lengths, w_uv, w_o, norm_gain, expert_ids, route_weights,
    w_gate, w_up, w_down,
):
    dma = pltpu.SemaphoreType.DMA
    vmem = pl.BlockSpec(memory_space=pltpu.VMEM)
    hbm = pl.BlockSpec(memory_space=pl.ANY)
    wide = max(w for _, w in PARTS)
    out = pl.pallas_call(
        layer,
        out_shape=jax.ShapeDtypeStruct((D // 128, 128), BF16),
        in_specs=[hbm] * 12,
        out_specs=vmem,
        scratch_shapes=[
            pltpu.SMEM((1,), jnp.int32),
            pltpu.SMEM((1, 8), jnp.int32),
            pltpu.SMEM((1, 8), F32),
            pltpu.VMEM((1, D), BF16),
            pltpu.VMEM((H, CW), BF16),
            pltpu.VMEM((1, D), F32),
            pltpu.VMEM((NCHUNK, CW, CHUNK), BF16),
            pltpu.VMEM((8, LAT, HD), BF16),
            pltpu.VMEM((D, FF), BF16),
            pltpu.VMEM((D, FF), BF16),
            pltpu.VMEM((FF, D), BF16),
            pltpu.VMEM((NCHUNK, H, CHUNK), F32),
            pltpu.VMEM((1, D), F32),
            pltpu.VMEM((16, 1, WIN), F32),
            pltpu.VMEM((8, 16, 8, WIN), BF16),
            pltpu.VMEM((8, 8, LAT + 128), BF16),
            pltpu.VMEM((8, 8, LAT + 128), BF16),
            pltpu.VMEM((8, 1152), BF16),
            pltpu.VMEM((16, 8, 1152), BF16),
            pltpu.VMEM((8, 16, WIN), BF16),
            pltpu.VMEM((8, 16, WIN), BF16),
            pltpu.VMEM((128, 128), F32),
            pltpu.VMEM((16, 8, 128), F32),
            pltpu.VMEM((4, 2, 4, 4, 4, 16, 128), BF16),
            pltpu.VMEM((1, D), F32),
            pltpu.VMEM((3, 64, wide), F32),
            pltpu.VMEM((3, 64, wide), BF16),
            pltpu.VMEM((3, 64, wide), BF16),
            pltpu.VMEM((3, 4, 16, wide), BF16),
            pltpu.VMEM((3, 3, 16, wide), BF16),
            pltpu.VMEM((16 * SPAN, 128), F32),
            pltpu.VMEM((3, 4, 4 * SPAN, 128), BF16),
            pltpu.VMEM((3, 3, 4 * SPAN, 128), BF16),
            pltpu.VMEM((3, 4, SPAN, 128), F32),
            pltpu.VMEM((3, 3, SPAN, 128), F32),
            pltpu.VMEM((D // 128, 128), F32),
            dma((NCHUNK + 11,)),
            dma((15,)), dma((15,)), dma((15,)), dma((15,)),
            dma((7,)), dma((7,)), dma((15,)), dma((15,)),
            dma((7,)), dma((7,)), dma((15,)), dma((15,)),
            dma((36,)), dma((36,)), dma((16,)), dma((16,)),
            dma((6,)), dma((6,)), dma((18,)), dma((18,)), dma((9,)), dma((9,)), dma((9,)), dma((9,)),
        ],
        compiler_params=pltpu.CompilerParams(
            collective_id=0, has_side_effects=True, vmem_limit_bytes=56 * 1024 * 1024
        ),
    )(
        lengths, expert_ids, route_weights, residual, query_latent, norm_gain.reshape(1, D),
        latent_cache.swapaxes(1, 2), w_uv, w_o, w_gate.reshape(D, FF), w_up.reshape(D, FF), w_down.reshape(FF, D),
    )
    return out.reshape(1, D)


def solution(mesh):
    return jax.shard_map(
        on_device,
        mesh=mesh,
        in_specs=(
            P(("dp", "tensor"), None),
            P(("dp", "tensor"), None, None),
            P(("dp", "tensor"), None, None),
            P(("dp", "tensor")),
            P("tensor", None, None),
            P("tensor", "dp", None),
            P(),
            P(("dp", "tensor"), None),
            P(("dp", "tensor"), None),
            P("dp", None, "tensor"),
            P("dp", None, "tensor"),
            P("dp", "tensor", None),
        ),
        out_specs=P(("dp", "tensor"), None),
        check_vma=False,
    )
```

time: 86.8 us -> 68.2 us (0.79)
  Pallas kernels: 76.8 us -> 66.1 us
  local copies, waits for them, and re-layouts: 9 us -> 1.34 us
    pallas_call x1, Pallas kernels: 76.8 us -> 66.1 us  [on_device(): pl.pallas_call(layer, out_shape=jax.ShapeDtypeStruct((D // 128, 128), BF1...]
    unnamed x2 -> x1, local copies, waits for them, and re-layouts: 9 us -> 1.34 us
where the time goes in v2:
time: 68.2 us; the launch traced here: 68.1 us
  Pallas kernels  66.1 us (97%)
  local copies, waits for them, and re-layouts  1.34 us (2%)
    pallas_call x1, Pallas kernels, on_device(): pl.pallas_call(layer, out_shape=jax.ShapeDtypeStruct((D // 128, 128), BF1...  66.1 us

profile of v2, /device:TPU:0, one launch (start us, length us, event | category | flops | bytes accessed | tf_op | source)
XLA Modules:
  0.0 68.1 jit_solution(2888562381736916871)
XLA Ops:
  0.7 66.1 %shard_map.118 = bf16[56,128]{1,0:T(8,128)(2,1)} custom-call(s32[1]{0:T(128)S(6)} %copy.16.len_hbm, s32[1,8]{1,0:T(1,128)} %ids_hbm.1, f32[1,8]{1,0:T(1,128)} %rw_hbm.1, bf16[1,7168]{1,0:T(2,128)(2,1)} %res_hbm.1, bf16[1,64,576]{2,1,0:T(8,128)(2,1)} %q_hbm.1, f32[1,7168]{1,0:T(1,128)} %bitcast.15, bf16[1,576,4096]{2,1,0:T(8,128)(2,1)} %bitcast.10, ...), custom_call_target="tpu_custom_call" | custom-call | tf_op jit(solution)/shard_map/pallas_call | solution.py:562
  66.7 1.3 %copy.15 = bf16[1,1,56,128]{3,1,2,0:T(2,128)(2,1)} copy(bf16[1,1,56,128]{3,2,1,0:T(8,128)(2,1)} %bitcast.14) | data formatting | bytes 28672

commit v3 on v2

--- a/solution.py
+++ b/solution.py
@@ -22,12 +22,14 @@
     (0, 0, 1280), (1, 0, 1280), (2, 0, 1280), (0, 1280, 1024), (1, 1280, 1024), (2, 1280, 1280),
 )
 ORDERS = (("z", "y", "x"), ("x", "z", "y"), ("y", "x", "z"))
-TILE_ORDER = ((0, 1, 2, 0), (1, 2, 0, 1))
+GATHER_ORDERS = (("z", "y", "x"), ("x", "z", "y"), ("x", "y", "z"))
+TILE_ORDER = ((0, 0, 1, 2), (2, 0, 1, 2))
 SPAN = 24
 PLANE = (
     (2, 2), (2, 1), (1, 2), (2, 3), (3, 2), (2, 0), (0, 2), (1, 1), (3, 3), (1, 3), (3, 1),
     (1, 0), (0, 1), (3, 0), (0, 3),
 )
+FIRST = 7
 LINE = ((2, 1), (2, 0), (1, 1), (3, 1), (1, 0), (3, 0), (0, 1))
 
 
@@ -53,10 +55,10 @@
     cache_v, wuv_v, wg_v, wu_v, wd_v,
     s_ref, resf_v, res_recv, wo_recv, lat_send, lat_recv, vals_send, vals_all,
     rs_send, rs_recv, st_send, st_recv, x_v, ig2_v,
-    d_own, c_send, c_recv, p1, p1r, q2f, q2, q2r, q3, q3r, mix_v,
+    d_own, c_send, c_recv, p1, p1r, q2f, q2, q2r, mix_v,
     local_sem, a2a_s, a2a_r, rb_s, rb_r, lat_s, lat_r, val_s, val_r,
     rs_s, rs_r, st_s, st_r, ag_s, ag_r, sib_s, sib_r,
-    cs_s, cs_r, p1_s, p1_r, p2_s, p2_r, p3_s, p3_r,
+    cs_s, cs_r, p1_s, p1_r, p2_s, p2_r,
 ):
     dp = lax.axis_index("dp")
     t = lax.axis_index("tensor")
@@ -66,14 +68,8 @@
     def dp_of(step):
         return lax.rem(pos["x"] + step[0], 4) * 4 + lax.rem(pos["y"] + step[1], 4)
 
-    def dp_before(step):
-        return lax.rem(pos["x"] + 4 - step[0], 4) * 4 + lax.rem(pos["y"] + 4 - step[1], 4)
-
     def t_of(step):
         return lax.rem(pos["z"] + step[0], 4) * 2 + lax.rem(core + step[1], 2)
-
-    def t_before(step):
-        return lax.rem(pos["z"] + 4 - step[0], 4) * 2 + lax.rem(core + step[1], 2)
 
     def at_dp(step):
         return {"dp": dp_of(step), "tensor": t}
@@ -86,6 +82,12 @@
         new[axis] = lax.rem(pos[axis] + i, 4)
         return {"dp": new["x"] * 4 + new["y"], "tensor": new["z"] * 2 + new["c"]}
 
+    def in_plane(a, b, step):
+        new = dict(pos)
+        new[a] = lax.rem(pos[a] + step[0], 4)
+        new[b] = lax.rem(pos[b] + step[1], 4)
+        return {"dp": new["x"] * 4 + new["y"], "tensor": new["z"] * 2 + new["c"]}
+
     sibling = {"dp": dp, "tensor": pos["z"] * 2 + (1 - core)}
 
     def remote(src, dst, ss, rs, dev):
@@ -93,18 +95,19 @@
             src_ref=src, dst_ref=dst, send_sem=ss, recv_sem=rs, device_id=dev, device_id_type=MESH
         )
 
-    def each(n, f):
-        def step(i, carry):
-            f(i)
-            return carry
-
-        lax.fori_loop(0, n, step, 0)
+    def sent(ref, sem):
+        remote(ref, ref, sem, sem, sibling).wait_send()
+
+    def arrived(ref, sem):
+        remote(ref, ref, sem, sem, sibling).wait_recv()
 
     barrier = pltpu.get_barrier_semaphore()
-    for step in PLANE:
-        pl.semaphore_signal(barrier, inc=1, device_id=at_dp(step), device_id_type=MESH)
-    for step in LINE:
-        pl.semaphore_signal(barrier, inc=1, device_id=at_t(step), device_id_type=MESH)
+    peers = [at_dp(step) for step in PLANE] + [at_t(step) for step in LINE]
+    for d in (1, 2, 3):
+        for e in (1, 2, 3):
+            peers += [in_plane("x", "z", (d, e)), in_plane("y", "z", (d, e))]
+    for peer in peers:
+        pl.semaphore_signal(barrier, inc=1, device_id=peer, device_id_type=MESH)
 
     def cache_copy(i):
         return pltpu.make_async_copy(
@@ -148,20 +151,23 @@
         return jnp.maximum(top, jnp.max(s, axis=1, keepdims=True))
 
     top = jnp.full((H, 1), MASKED, F32)
-    for i in range(NCHUNK // 2):
+    for i in range(NCHUNK):
         top = score(i, top)
 
     small[2].wait()
     resf_v[...] = res_ref[...].astype(F32)
-    pl.semaphore_wait(barrier, 22)
+    pl.semaphore_wait(barrier, 40)
 
     def wo_copy(n, src_dp, slot, skip):
         first = pl.multiple_of(window_start(src_dp) + skip, 128)
         return remote(
             wo_hbm.at[:, :, pl.ds(first, WIN - skip)],
             wo_recv.at[:, slot, :, pl.ds(skip, WIN - skip)],
-            a2a_s.at[n], a2a_r.at[n], at_dp(PLANE[n]),
-        )
+            a2a_s.at[skip // 128], a2a_r, at_dp(PLANE[n]),
+        )
+
+    def wo_blocks(n, skip):
+        return wo_recv.at[:, pl.ds(0, n), :, pl.ds(skip, WIN - skip)]
 
     def by_parity(odd, f):
         pl.when(odd == 0)(lambda: f(0))
@@ -170,21 +176,20 @@
     def res_copy(n):
         first = pl.multiple_of(window_start(dp_of(PLANE[n])), 128)
         return remote(
-            resf_v.at[:, pl.ds(first, WIN)], res_recv.at[dp],
-            rb_s.at[n], rb_r.at[n], at_dp(PLANE[n]),
-        )
-
-    for n, step in enumerate(PLANE):
-        by_parity(
-            lax.rem(dp_of(step), 2),
-            lambda skip, n=n, step=step: wo_copy(n, dp_of(step), dp, skip).start(),
-        )
+            resf_v.at[:, pl.ds(first, WIN)], res_recv.at[dp], rb_s, rb_r, at_dp(PLANE[n])
+        )
+
+    def send_wo(steps):
+        for n in steps:
+            to = dp_of(PLANE[n])
+            by_parity(
+                lax.rem(to, 2), lambda skip, n=n, to=to: wo_copy(n, to, dp, skip).start()
+            )
+
+    send_wo(range(FIRST))
     res_recv[dp] = resf_v[:, pl.ds(start, WIN)]
     for n in range(15):
         res_copy(n).start()
-
-    for i in range(NCHUNK // 2, NCHUNK):
-        top = score(i, top)
 
     w_copies = [local(8 + k, src, dst) for k, (src, dst) in enumerate(
         ((wg_hbm, wg_v), (wu_hbm, wu_v), (wd_hbm, wd_v)))]
@@ -216,12 +221,8 @@
 
     def lat_copy(n):
         return remote(
-            lat_send.at[t_of(LINE[n])], lat_recv.at[t], lat_s.at[n], lat_r.at[n], at_t(LINE[n])
-        )
-
-    def lat_wait(n):
-        src = t_before(LINE[n])
-        remote(lat_send.at[src], lat_recv.at[src], lat_s.at[n], lat_r.at[n], at_t(LINE[n])).wait_recv()
+            lat_send.at[t_of(LINE[n])], lat_recv.at[t], lat_s, lat_r, at_t(LINE[n])
+        )
 
     for n in range(7):
         lat_copy(n).start()
@@ -230,8 +231,7 @@
     gain = gain_ref[...]
     ig2_v[...] = 1.0 / (gain * gain)
     wuv_copy.wait()
-    for n in range(7):
-        lat_wait(n)
+    arrived(lat_recv.at[pl.ds(0, 7)], lat_r)
 
     by_head = onehot(64, lambda r: jnp.bitwise_and(r, 7) * 8 + jnp.right_shift(r, 3))
     lat = lat_recv[...].astype(F32).reshape(64, LAT + 128).astype(BF16)
@@ -240,26 +240,31 @@
     pieces.append(lat[0:8, LAT:])
     vals_send[...] = jnp.concatenate(pieces, axis=1).astype(BF16)
 
-    def val_copy(n):
-        return remote(vals_send, vals_all.at[dp], val_s.at[n], val_r.at[n], at_dp(PLANE[n]))
-
-    def val_wait(n):
-        src = dp_before(PLANE[n])
-        remote(vals_send, vals_all.at[src], val_s.at[n], val_r.at[n], at_dp(PLANE[n])).wait_recv()
-
-    for n in range(15):
-        val_copy(n).start()
-    vals_all[dp] = vals_send[...]
+    v1 = pos["x"] + core * (pos["y"] - pos["x"])
+    v2 = pos["x"] + pos["y"] - v1
+
+    def val_copy(k, i):
+        here = vals_all.at[v2] if k else vals_all.at[v2, v1]
+        dx = (1 - core) * i if k == 0 else core * i
+        return remote(here, here, val_s.at[k], val_r.at[k], at_dp((dx, i - dx)))
+
+    vals_all[v2, v1] = vals_send[...]
+    for i in (2, 1, 3):
+        val_copy(0, i).start()
+    send_wo(range(FIRST, 15))
+    arrived(vals_all.at[0, pl.ds(0, 3)], val_r.at[0])
+    for i in (2, 1, 3):
+        val_copy(1, i).start()
     own_wo.wait()
-    for n in range(15):
-        by_parity(
-            lax.rem(dp, 2),
-            lambda skip, n=n: wo_copy(n, dp, dp_before(PLANE[n]), skip).wait_recv(),
-        )
-    for n in range(15):
-        val_wait(n)
-
-    to_t_order = onehot(128, lambda r: jnp.bitwise_and(r, 15) * 8 + jnp.right_shift(r, 4))
+    by_parity(lax.rem(dp, 2), lambda skip: arrived(wo_blocks(15, skip), a2a_r))
+    arrived(vals_all.at[pl.ds(0, 3)], val_r.at[1])
+
+    def from_row(r, row_t):
+        x, y = jnp.bitwise_and(jnp.right_shift(r, 2), 3), jnp.bitwise_and(r, 3)
+        inner = x + core * (y - x)
+        return (x + y - inner) * 32 + inner * 8 + row_t
+
+    to_t_order = onehot(128, lambda r: from_row(r, jnp.right_shift(r, 4)))
     vals_raw = vals_all[...].astype(F32).reshape(128, 1152).astype(BF16)
     vals = dot(to_t_order, vals_raw[:, : 8 * HD]).astype(BF16)
     part = jnp.zeros((128, WIN), F32)
@@ -271,12 +276,8 @@
 
     def rs_copy(n):
         return remote(
-            rs_send.at[t_of(LINE[n])], rs_recv.at[t], rs_s.at[n], rs_r.at[n], at_t(LINE[n])
-        )
-
-    def rs_wait(n):
-        src = t_before(LINE[n])
-        remote(rs_send.at[src], rs_recv.at[src], rs_s.at[n], rs_r.at[n], at_t(LINE[n])).wait_recv()
+            rs_send.at[t_of(LINE[n])], rs_recv.at[t], rs_s, rs_r, at_t(LINE[n])
+        )
 
     for n in range(7):
         rs_copy(n).start()
@@ -284,25 +285,19 @@
 
     to_c_order = onehot(
         128,
-        lambda r: jnp.bitwise_and(r, 15) * 8
-        + jnp.bitwise_and(jnp.right_shift(r, 4), 3) * 2
-        + jnp.right_shift(r, 6),
+        lambda r: from_row(
+            r, jnp.bitwise_and(jnp.right_shift(r, 4), 3) * 2 + jnp.right_shift(r, 6)
+        ),
     )
     coefs = dot(to_c_order, vals_raw[:, 8 * HD :])
     col = lax.broadcasted_iota(jnp.int32, (128, 128), 1)
     mine = (col == dp) | (col == dp + 16)
     coef_col = jnp.sum(jnp.where(mine, coefs, 0.0), axis=1, keepdims=True)
 
-    for n in range(15):
-        src = dp_before(PLANE[n])
-        remote(
-            resf_v.at[:, pl.ds(start, WIN)], res_recv.at[src],
-            rb_s.at[n], rb_r.at[n], at_dp(PLANE[n]),
-        ).wait_recv()
+    arrived(res_recv.at[pl.ds(0, 15)], rb_r)
     res = jnp.concatenate([res_recv[k] for k in range(16)], axis=0)
 
-    for n in range(7):
-        rs_wait(n)
+    arrived(rs_recv.at[pl.ds(0, 7)], rs_r)
     stream = res
     for k in range(8):
         stream = stream + rs_recv[k].astype(F32)
@@ -313,7 +308,7 @@
         return zero + c * (one - zero)
 
     def axis_of(j, c, k):
-        return ORDERS[TILE_ORDER[c][j]][k]
+        return GATHER_ORDERS[TILE_ORDER[c][j]][k]
 
     def place(j, k, c):
         return either(c, lambda v: pos[axis_of(j, v, k)])
@@ -329,26 +324,52 @@
             for name in ("dp", "tensor")
         }
 
-    def gather(j, phase, i):
-        here = block(j, phase, core, 0)
-        n = (j * 3 + phase) * 3 + i - 1
-        return remote(here, here, ag_s.at[n], ag_r.at[n], partner(j, phase, i))
-
-    def gather_wait(j, phase, i):
-        there = block(j, phase, core, i)
-        n = (j * 3 + phase) * 3 + i - 1
-        remote(there, there, ag_s.at[n], ag_r.at[n], partner(j, phase, i)).wait_recv()
-
-    def to_sibling(j, i, c):
-        there = block(j, 2, c, i)
-        return remote(there, there, sib_s.at[j * 4 + i], sib_r.at[j * 4 + i], sibling)
+    def spread(j):
+        def go():
+            here = x_v.at[j, core, place(j, 2, core), place(j, 1, core), place(j, 0, core)]
+            for step in PLANE:
+                target = {
+                    name: either(
+                        core,
+                        lambda v, name=name: in_plane(axis_of(j, v, 0), axis_of(j, v, 1), step)[name],
+                    )
+                    for name in ("dp", "tensor")
+                }
+                remote(
+                    here, here, ag_s.at[0 if j else 1], ag_r.at[j * 7 + step[1]], target
+                ).start()
+
+        if j == 0:
+            pl.when(lax.rem(pos["y"], 2) == 0)(go)
+        else:
+            go()
+
+    def rows_on(j, back):
+        def go():
+            n = 4 if back else 3
+            arrived(x_v.at[0, 0, 0, 0, pl.ds(0, n)], ag_r.at[j * 7 + back])
+            row = lax.rem(place(j, 1, core) - back + 4, 4)
+            here = x_v.at[j, core, place(j, 2, core), row]
+            for i in (2, 1, 3):
+                remote(
+                    here, here, ag_s.at[3 if j == 0 else 2], ag_r.at[j * 7 + 3 + i], partner(j, 2, i)
+                ).start()
+
+        if j == 0:
+            pl.when(lax.rem(pos["y"] - back + 4, 2) == 0)(go)
+        else:
+            go()
+
+    def to_sibling(j, i):
+        there = block(j, 2, core, i)
+        return remote(there, there, sib_s, sib_r, sibling)
 
     for j in range(4):
         x_v[j, core, place(j, 2, core), place(j, 1, core), place(j, 0, core)] = scaled[
             :, 128 * j : 128 * j + 128
         ]
-        for i in (2, 1, 3):
-            gather(j, 0, i).start()
+    for j in (1, 2, 3, 0):
+        spread(j)
 
     st_send[...] = jnp.zeros_like(st_send)
     for j in range(4):
@@ -358,44 +379,34 @@
     def st_copy(n):
         there = pl.multiple_of(dp_of(PLANE[n]) * 8, 8)
         return remote(
-            st_send.at[pl.ds(there, 8)], st_recv.at[dp], st_s.at[n], st_r.at[n], at_dp(PLANE[n])
-        )
-
-    def st_wait(n):
-        src = dp_before(PLANE[n])
-        remote(
-            st_send.at[pl.ds(0, 8)], st_recv.at[src], st_s.at[n], st_r.at[n], at_dp(PLANE[n])
-        ).wait_recv()
-
-    for phase in (1, 2):
-        for j in range(4):
-            for i in (1, 3, 2):
-                gather_wait(j, phase - 1, i)
-            for i in (2, 1, 3):
-                gather(j, phase, i).start()
-            if phase == 2:
-                to_sibling(j, 0, core).start()
+            st_send.at[pl.ds(there, 8)], st_recv.at[dp], st_s, st_r, at_dp(PLANE[n])
+        )
+
+    for back in (0, 1, 3, 2):
+        for j in (1, 2, 3, 0):
+            rows_on(j, back)
+    for j in (1, 2, 3, 0):
+        to_sibling(j, 0).start()
 
     for n in range(15):
         st_copy(n).start()
-    for n in range(15):
-        by_parity(
-            lax.rem(dp_of(PLANE[n]), 2),
-            lambda skip, n=n: wo_copy(n, dp_of(PLANE[n]), dp, skip).wait_send(),
-        )
-        res_copy(n).wait_send()
-        val_copy(n).wait_send()
-    for n in range(7):
-        lat_copy(n).wait_send()
-        rs_copy(n).wait_send()
+
+    def wo_sent(skip):
+        for n, other in ((7, skip), (8, 128 - skip)):
+            sent(wo_blocks(n, other), a2a_s.at[other // 128])
+
+    by_parity(lax.rem(dp, 2), wo_sent)
+    sent(res_recv.at[pl.ds(0, 15)], rb_s)
+    sent(vals_all.at[0, pl.ds(0, 3)], val_s.at[0])
+    sent(vals_all.at[pl.ds(0, 3)], val_s.at[1])
+    sent(lat_recv.at[pl.ds(0, 7)], lat_s)
+    sent(rs_recv.at[pl.ds(0, 7)], rs_s)
 
     for i in (1, 3, 2):
-        for j in range(4):
-            gather_wait(j, 2, i)
-            to_sibling(j, i, core).start()
-    for i in (0, 1, 3, 2):
-        for j in range(4):
-            to_sibling(j, i, 1 - core).wait_recv()
+        for j in (0, 1, 2, 3):
+            arrived(x_v.at[0, 0, 0] if j else x_v.at[0, 0, 0, pl.ds(0, 2)], ag_r.at[j * 7 + 3 + i])
+            to_sibling(j, i).start()
+    arrived(x_v.at[:, 0], sib_r)
     for copy in w_copies:
         copy.wait()
 
@@ -403,7 +414,7 @@
         halves = []
         for c in range(2):
             at = {"x": x, "y": y, "z": slice(None)}
-            i1, i2, i3 = (at[a] for a in ORDERS[TILE_ORDER[c][j]])
+            i1, i2, i3 = (at[a] for a in GATHER_ORDERS[TILE_ORDER[c][j]])
             halves.append(x_v[j, c, i3, i2, i1].reshape(64, 128))
         return jnp.concatenate(halves, axis=0)
 
@@ -443,17 +454,16 @@
         p, at, w = PIECES[s]
         cols = pl.ds(at, w)
         return remote(
-            c_send.at[p, :, cols], c_recv.at[p, :, cols], cs_s.at[s], cs_r.at[s], sibling
+            c_send.at[p, :, cols], c_recv.at[p, :, cols], cs_s, cs_r.at[s], sibling
         )
 
     def sum1(s, i):
         p, at, w = PIECES[s]
         axis = ORDERS[p][0]
-        n = s * 3 + i - 1
         cols = pl.ds(at, w)
         return remote(
             p1.at[p, lax.rem(pos[axis] + i, 4), :, cols], p1r.at[p, i - 1, :, cols],
-            p1_s.at[n], p1_r.at[n], along(axis, i),
+            p1_s, p1_r.at[p], along(axis, i),
         )
 
     def down(s):
@@ -472,83 +482,62 @@
         for i in (2, 1, 3):
             sum1(s, i).start()
 
-    down(0)
-    for s in range(1, 6):
-        down(s)
-        pair(s - 1)
-    pair(5)
-
-    def sum2(p, i):
-        axis = ORDERS[p][1]
-        n = p * 3 + i - 1
-        return remote(
-            q2.at[p, lax.rem(pos[axis] + i, 4)], q2r.at[p, i - 1], p2_s.at[n], p2_r.at[n], along(axis, i)
+    for s in range(len(PIECES) + 2):
+        if s < len(PIECES):
+            down(s)
+        if s >= 2:
+            pair(s - 2)
+
+    def my_row(p):
+        return pos[ORDERS[p][1]] * 4 + pos[ORDERS[p][2]]
+
+    def row_copy(p, step):
+        a, b = ORDERS[p][1], ORDERS[p][2]
+        there = lax.rem(pos[a] + step[0], 4) * 4 + lax.rem(pos[b] + step[1], 4)
+        return remote(
+            q2.at[p, there], q2r.at[p, my_row(p)], p2_s, p2_r.at[p], in_plane(a, b, step)
         )
 
     q2f[...] = jnp.zeros_like(q2f)
     for p, (first, w) in enumerate(PARTS):
-        for s in (p, p + 3):
-            for i in (1, 3, 2):
-                sum1(s, i).wait_recv()
+        arrived(p1r.at[p, :, :, pl.ds(0, w)], p1_r.at[p])
         o = p1[p, pos[ORDERS[p][0]], :, 0:w].astype(F32)
         for i in range(3):
             o = o + p1r[p, i, :, 0:w].astype(F32)
         for j in range(w // 128):
             q2f[pl.ds(j, 16, stride=SPAN), :] = o[:, 128 * j : 128 * j + 128]
-        q2[p] = q2f[...].astype(BF16).reshape(4, 4 * SPAN, 128)
-        for i in (2, 1, 3):
-            sum2(p, i).start()
-
-    def sum3(p, i):
-        axis = ORDERS[p][2]
-        n = p * 3 + i - 1
-        return remote(
-            q3.at[p, lax.rem(pos[axis] + i, 4)], q3r.at[p, i - 1], p3_s.at[n], p3_r.at[n], along(axis, i)
-        )
-
-    for n in range(15):
-        st_wait(n)
-        st_copy(n).wait_send()
+        q2[p] = q2f[...].reshape(16, SPAN, 128).astype(BF16)
+        for step in PLANE:
+            row_copy(p, step).start()
+        q2r[p, my_row(p)] = q2[p, my_row(p)]
+
+    arrived(st_recv.at[pl.ds(0, 15)], st_r)
+    sent(st_recv.at[pl.ds(0, 15)], st_s)
     for k in range(8):
         mix_v[7 * k : 7 * k + 4, :] = st_recv[2 * k, 0:4, :]
         mix_v[7 * k + 4 : 7 * k + 7, :] = st_recv[2 * k + 1, 1:4, :]
 
-    for p in range(3):
-        for i in (1, 3, 2):
-            sum2(p, i).wait_recv()
-        o = q2[p, pos[ORDERS[p][1]]].astype(F32)
-        for i in range(3):
+    sent(q2f.at[pl.ds(0, 360)], ag_s.at[0])
+
+    @pl.when(lax.rem(pos["y"], 2) == 0)
+    def _():
+        sent(q2f.at[pl.ds(0, 120)], ag_s.at[1])
+
+    sent(x_v.at[pl.ds(0, 3), 0, pl.ds(0, 3)], ag_s.at[2])
+    sent(x_v.at[pl.ds(0, 2), 0, 0, pl.ds(0, 3)], ag_s.at[3])
+    sent(x_v.at[:, 0], sib_s)
+    sent(wd_v.at[pl.ds(0, 64)], cs_s)
+    sent(wd_v.at[pl.ds(0, 48)], p1_s)
+
+    for p, (first, w) in enumerate(PARTS):
+        arrived(q2r.at[p, pl.ds(0, 15)], p2_r.at[p])
+        o = q2r[p, 0].astype(F32)
+        for i in range(1, 16):
             o = o + q2r[p, i].astype(F32)
-        q3[p] = o.reshape(4, SPAN, 128)
-        for i in (2, 1, 3):
-            sum3(p, i).start()
-
-    for j in range(4):
-        for phase in range(3):
-            for i in (1, 2, 3):
-                gather(j, phase, i).wait_send()
-        for i in range(4):
-            to_sibling(j, i, core).wait_send()
-    for s in range(6):
-        core_copy(s).wait_send()
-        for i in (1, 2, 3):
-            sum1(s, i).wait_send()
-    for p in range(3):
-        for i in (1, 2, 3):
-            sum2(p, i).wait_send()
-
-    for p, (first, w) in enumerate(PARTS):
-        for i in (1, 3, 2):
-            sum3(p, i).wait_recv()
-        o = q3[p, pos[ORDERS[p][2]]]
-        for i in range(3):
-            o = o + q3r[p, i]
         tiles = slice(first // 128, (first + w) // 128)
         mix_v[tiles, :] = mix_v[tiles, :] + o[: w // 128]
     out_ref[...] = mix_v[...].astype(BF16)
-    for p in range(3):
-        for i in (1, 2, 3):
-            sum3(p, i).wait_send()
+    sent(q2r.at[:, pl.ds(0, 15)], p2_s)
 
 
 def on_device(
@@ -583,7 +572,7 @@
             pltpu.VMEM((8, 8, LAT + 128), BF16),
             pltpu.VMEM((8, 8, LAT + 128), BF16),
             pltpu.VMEM((8, 1152), BF16),
-            pltpu.VMEM((16, 8, 1152), BF16),
+            pltpu.VMEM((4, 4, 8, 1152), BF16),
             pltpu.VMEM((8, 16, WIN), BF16),
             pltpu.VMEM((8, 16, WIN), BF16),
             pltpu.VMEM((128, 128), F32),
@@ -596,17 +585,13 @@
             pltpu.VMEM((3, 4, 16, wide), BF16),
             pltpu.VMEM((3, 3, 16, wide), BF16),
             pltpu.VMEM((16 * SPAN, 128), F32),
-            pltpu.VMEM((3, 4, 4 * SPAN, 128), BF16),
-            pltpu.VMEM((3, 3, 4 * SPAN, 128), BF16),
-            pltpu.VMEM((3, 4, SPAN, 128), F32),
-            pltpu.VMEM((3, 3, SPAN, 128), F32),
+            pltpu.VMEM((3, 16, SPAN, 128), BF16),
+            pltpu.VMEM((3, 16, SPAN, 128), BF16),
             pltpu.VMEM((D // 128, 128), F32),
             dma((NCHUNK + 11,)),
-            dma((15,)), dma((15,)), dma((15,)), dma((15,)),
-            dma((7,)), dma((7,)), dma((15,)), dma((15,)),
-            dma((7,)), dma((7,)), dma((15,)), dma((15,)),
-            dma((36,)), dma((36,)), dma((16,)), dma((16,)),
-            dma((6,)), dma((6,)), dma((18,)), dma((18,)), dma((9,)), dma((9,)), dma((9,)), dma((9,)),
+            dma((2,)), dma, dma, dma, dma, dma, dma((2,)), dma((2,)),
+            dma, dma, dma, dma, dma((4,)), dma((28,)), dma, dma,
+            dma, dma((6,)), dma, dma((3,)), dma, dma((3,)),
         ],
         compiler_params=pltpu.CompilerParams(
             collective_id=0, has_side_effects=True, vmem_limit_bytes=56 * 1024 * 1024

time: 68.2 us -> 60.8 us (0.89)
  Pallas kernels: 66.1 us -> 58.2 us
    pallas_call x1, Pallas kernels: 66.1 us -> 58.2 us  [on_device(): pl.pallas_call(layer, out_shape=jax.ShapeDtypeStruct((D // 128, 128), BF1...]
where the time goes in v3:
time: 60.8 us; the launch traced here: 60.2 us
  Pallas kernels  58.2 us (96%)
  local copies, waits for them, and re-layouts  1.34 us (2%)
  between operations  0.66 us (1%)
    pallas_call x1, Pallas kernels, on_device(): pl.pallas_call(layer, out_shape=jax.ShapeDtypeStruct((D // 128, 128), BF1...  58.2 us
    unnamed x1, local copies, waits for them, and re-layouts  1.34 us

profile of v3, /device:TPU:0, one launch (start us, length us, event | category | flops | bytes accessed | tf_op | source)
XLA Modules:
  0.0 60.2 jit_solution(5994242738932709472)
XLA Ops:
  0.7 58.2 %shard_map.118 = bf16[56,128]{1,0:T(8,128)(2,1)} custom-call(s32[1]{0:T(128)S(6)} %copy.16.len_hbm, s32[1,8]{1,0:T(1,128)} %ids_hbm.1, f32[1,8]{1,0:T(1,128)} %rw_hbm.1, bf16[1,7168]{1,0:T(2,128)(2,1)} %res_hbm.1, bf16[1,64,576]{2,1,0:T(8,128)(2,1)} %q_hbm.1, f32[1,7168]{1,0:T(1,128)} %bitcast.15, bf16[1,576,4096]{2,1,0:T(8,128)(2,1)} %bitcast.10, ...), custom_call_target="tpu_custom_call" | custom-call | tf_op jit(solution)/shard_map/pallas_call | solution.py:551
  58.9 1.3 %copy.15 = bf16[1,1,56,128]{3,1,2,0:T(2,128)(2,1)} copy(bf16[1,1,56,128]{3,2,1,0:T(8,128)(2,1)} %bitcast.14) | data formatting | bytes 28672

commit v4 on v3

--- a/solution.py
+++ b/solution.py
@@ -14,22 +14,22 @@
 CHUNK = 1024
 NCHUNK = CTX // CHUNK
 WIN = 512
+HALF = 256
 SCALE = 192 ** (-0.5)
 EPS = 1e-06
 MASKED = -1e30
-PARTS = ((0, 2304), (2304, 2304), (4608, 2560))
-PIECES = (
-    (0, 0, 1280), (1, 0, 1280), (2, 0, 1280), (0, 1280, 1024), (1, 1280, 1024), (2, 1280, 1280),
-)
+PARTS = ((0, 2432), (2432, 2432), (4864, 2304))
+DIRECT = 768
+PIECES = ((0, 768, 1664), (1, 768, 1664), (2, 768, 1536))
 ORDERS = (("z", "y", "x"), ("x", "z", "y"), ("y", "x", "z"))
 GATHER_ORDERS = (("z", "y", "x"), ("x", "z", "y"), ("x", "y", "z"))
-TILE_ORDER = ((0, 0, 1, 2), (2, 0, 1, 2))
+TILE_ORDER = ((2, 0, 0, 1), (0, 1, 2, 2))
 SPAN = 24
 PLANE = (
     (2, 2), (2, 1), (1, 2), (2, 3), (3, 2), (2, 0), (0, 2), (1, 1), (3, 3), (1, 3), (3, 1),
     (1, 0), (0, 1), (3, 0), (0, 3),
 )
-FIRST = 7
+FIRST = 5
 LINE = ((2, 1), (2, 0), (1, 1), (3, 1), (1, 0), (3, 0), (0, 1))
 
 
@@ -55,10 +55,10 @@
     cache_v, wuv_v, wg_v, wu_v, wd_v,
     s_ref, resf_v, res_recv, wo_recv, lat_send, lat_recv, vals_send, vals_all,
     rs_send, rs_recv, st_send, st_recv, x_v, ig2_v,
-    d_own, c_send, c_recv, p1, p1r, q2f, q2, q2r, mix_v,
+    d_own, c_send, c_recv, p1, p1r, q2f, q2, q2r, mix_v, order_v, pd, pdr,
     local_sem, a2a_s, a2a_r, rb_s, rb_r, lat_s, lat_r, val_s, val_r,
     rs_s, rs_r, st_s, st_r, ag_s, ag_r, sib_s, sib_r,
-    cs_s, cs_r, p1_s, p1_r, p2_s, p2_r,
+    cs_s, cs_r, p1_s, p1_r, p2_s, p2_r, pd_s, pd_r,
 ):
     dp = lax.axis_index("dp")
     t = lax.axis_index("tensor")
@@ -88,6 +88,9 @@
         new[b] = lax.rem(pos[b] + step[1], 4)
         return {"dp": new["x"] * 4 + new["y"], "tensor": new["z"] * 2 + new["c"]}
 
+    def crossed(device):
+        return {"dp": device["dp"], "tensor": device["tensor"] + 1 - 2 * core}
+
     sibling = {"dp": dp, "tensor": pos["z"] * 2 + (1 - core)}
 
     def remote(src, dst, ss, rs, dev):
@@ -106,6 +109,7 @@
     for d in (1, 2, 3):
         for e in (1, 2, 3):
             peers += [in_plane("x", "z", (d, e)), in_plane("y", "z", (d, e))]
+        peers += [crossed(along("x", d)), crossed(along("y", d))]
     for peer in peers:
         pl.semaphore_signal(barrier, inc=1, device_id=peer, device_id_type=MESH)
 
@@ -156,18 +160,17 @@
 
     small[2].wait()
     resf_v[...] = res_ref[...].astype(F32)
-    pl.semaphore_wait(barrier, 40)
-
-    def wo_copy(n, src_dp, slot, skip):
-        first = pl.multiple_of(window_start(src_dp) + skip, 128)
-        return remote(
-            wo_hbm.at[:, :, pl.ds(first, WIN - skip)],
-            wo_recv.at[:, slot, :, pl.ds(skip, WIN - skip)],
-            a2a_s.at[skip // 128], a2a_r, at_dp(PLANE[n]),
-        )
-
-    def wo_blocks(n, skip):
-        return wo_recv.at[:, pl.ds(0, n), :, pl.ds(skip, WIN - skip)]
+    pl.semaphore_wait(barrier, 46)
+
+    def wo_copy(n, src_dp, slot, lo, hi, ss, rs):
+        first = pl.multiple_of(window_start(src_dp) + lo, 128)
+        return remote(
+            wo_hbm.at[:, :, pl.ds(first, hi - lo)], wo_recv.at[:, slot, :, pl.ds(lo, hi - lo)],
+            ss, rs, at_dp(PLANE[n]),
+        )
+
+    def wo_blocks(n, lo, hi):
+        return wo_recv.at[:, pl.ds(0, n), :, pl.ds(lo, hi - lo)]
 
     def by_parity(odd, f):
         pl.when(odd == 0)(lambda: f(0))
@@ -179,18 +182,19 @@
             resf_v.at[:, pl.ds(first, WIN)], res_recv.at[dp], rb_s, rb_r, at_dp(PLANE[n])
         )
 
-    def send_wo(steps):
+    def send_low(steps):
         for n in steps:
             to = dp_of(PLANE[n])
             by_parity(
-                lax.rem(to, 2), lambda skip, n=n, to=to: wo_copy(n, to, dp, skip).start()
+                lax.rem(to, 2),
+                lambda skip, n=n, to=to: wo_copy(
+                    n, to, dp, skip, HALF, a2a_s.at[skip // 128], a2a_r.at[0]
+                ).start(),
             )
 
-    send_wo(range(FIRST))
+    for n in range(15):
+        wo_copy(n, dp_of(PLANE[n]), dp, HALF, WIN, a2a_s.at[2], a2a_r.at[1]).start()
     res_recv[dp] = resf_v[:, pl.ds(start, WIN)]
-    for n in range(15):
-        res_copy(n).start()
-
     w_copies = [local(8 + k, src, dst) for k, (src, dst) in enumerate(
         ((wg_hbm, wg_v), (wu_hbm, wu_v), (wd_hbm, wd_v)))]
     for copy in w_copies:
@@ -227,15 +231,17 @@
     for n in range(7):
         lat_copy(n).start()
     lat_recv[t] = lat_send[t]
+    order_v[0, :64, :64] = onehot(
+        64, lambda r: jnp.bitwise_and(r, 7) * 8 + jnp.right_shift(r, 3)
+    )
     small[3].wait()
     gain = gain_ref[...]
     ig2_v[...] = 1.0 / (gain * gain)
     wuv_copy.wait()
     arrived(lat_recv.at[pl.ds(0, 7)], lat_r)
 
-    by_head = onehot(64, lambda r: jnp.bitwise_and(r, 7) * 8 + jnp.right_shift(r, 3))
     lat = lat_recv[...].astype(F32).reshape(64, LAT + 128).astype(BF16)
-    lat = dot(by_head, lat)
+    lat = dot(order_v[0, :64, :64], lat)
     pieces = [dot(lat[8 * h : 8 * h + 8, :LAT].astype(BF16), wuv_v[h]) for h in range(8)]
     pieces.append(lat[0:8, LAT:])
     vals_send[...] = jnp.concatenate(pieces, axis=1).astype(BF16)
@@ -251,57 +257,69 @@
     vals_all[v2, v1] = vals_send[...]
     for i in (2, 1, 3):
         val_copy(0, i).start()
-    send_wo(range(FIRST, 15))
-    arrived(vals_all.at[0, pl.ds(0, 3)], val_r.at[0])
-    for i in (2, 1, 3):
-        val_copy(1, i).start()
-    own_wo.wait()
-    by_parity(lax.rem(dp, 2), lambda skip: arrived(wo_blocks(15, skip), a2a_r))
-    arrived(vals_all.at[pl.ds(0, 3)], val_r.at[1])
-
+    send_low(range(FIRST))
     def from_row(r, row_t):
         x, y = jnp.bitwise_and(jnp.right_shift(r, 2), 3), jnp.bitwise_and(r, 3)
         inner = x + core * (y - x)
         return (x + y - inner) * 32 + inner * 8 + row_t
 
-    to_t_order = onehot(128, lambda r: from_row(r, jnp.right_shift(r, 4)))
-    vals_raw = vals_all[...].astype(F32).reshape(128, 1152).astype(BF16)
-    vals = dot(to_t_order, vals_raw[:, : 8 * HD]).astype(BF16)
-    part = jnp.zeros((128, WIN), F32)
-    for h in range(8):
-        part = part + dot(
-            vals[:, h * HD : (h + 1) * HD], wo_recv[h].astype(F32).reshape(128, WIN).astype(BF16)
-        )
-    rs_send[...] = part.astype(BF16).reshape(8, 16, WIN)
-
-    def rs_copy(n):
-        return remote(
-            rs_send.at[t_of(LINE[n])], rs_recv.at[t], rs_s, rs_r, at_t(LINE[n])
-        )
-
-    for n in range(7):
-        rs_copy(n).start()
-    rs_recv[t] = rs_send[t]
-
-    to_c_order = onehot(
+    order_v[1] = onehot(128, lambda r: from_row(r, jnp.right_shift(r, 4)))
+    order_v[2] = onehot(
         128,
         lambda r: from_row(
             r, jnp.bitwise_and(jnp.right_shift(r, 4), 3) * 2 + jnp.right_shift(r, 6)
         ),
     )
-    coefs = dot(to_c_order, vals_raw[:, 8 * HD :])
+    bits = {"c": 6, "z": 4, "x": 2, "y": 0}
+    for p in range(3):
+
+        def source(r):
+            src = jnp.left_shift(jnp.bitwise_xor(jnp.right_shift(r, 6), core), bits["c"])
+            for a, shift in zip(ORDERS[p], (4, 2, 0)):
+                src = src + jnp.left_shift(jnp.bitwise_and(jnp.right_shift(r, shift), 3), bits[a])
+            return src
+
+        order_v[3 + p] = onehot(128, source)
+    arrived(vals_all.at[0, pl.ds(0, 3)], val_r.at[0])
+    for i in (2, 1, 3):
+        val_copy(1, i).start()
+    send_low(range(FIRST, 15))
+    for n in range(15):
+        res_copy(n).start()
+    own_wo.wait()
+    arrived(wo_blocks(15, HALF, WIN), a2a_r.at[1])
+    arrived(vals_all.at[pl.ds(0, 3)], val_r.at[1])
+
+    vals_raw = vals_all[...].astype(F32).reshape(128, 1152).astype(BF16)
+    vals = dot(order_v[1], vals_raw[:, : 8 * HD]).astype(BF16)
+
+    def rs_copy(half, n):
+        return remote(
+            rs_send.at[half, t_of(LINE[n])], rs_recv.at[half, t],
+            rs_s.at[half], rs_r.at[half], at_t(LINE[n]),
+        )
+
+    def project(half):
+        part = jnp.zeros((128, HALF), F32)
+        for h in range(8):
+            w = wo_recv[h, :, :, half * HALF : half * HALF + HALF]
+            part = part + dot(
+                vals[:, h * HD : (h + 1) * HD], w.astype(F32).reshape(128, HALF).astype(BF16)
+            )
+        rs_send[half] = part.astype(BF16).reshape(8, 16, HALF)
+        for n in range(7):
+            rs_copy(half, n).start()
+        rs_recv[half, t] = rs_send[half, t]
+
+    project(1)
+
+    coefs = dot(order_v[2], vals_raw[:, 8 * HD :])
     col = lax.broadcasted_iota(jnp.int32, (128, 128), 1)
     mine = (col == dp) | (col == dp + 16)
     coef_col = jnp.sum(jnp.where(mine, coefs, 0.0), axis=1, keepdims=True)
 
-    arrived(res_recv.at[pl.ds(0, 15)], rb_r)
-    res = jnp.concatenate([res_recv[k] for k in range(16)], axis=0)
-
-    arrived(rs_recv.at[pl.ds(0, 7)], rs_r)
-    stream = res
-    for k in range(8):
-        stream = stream + rs_recv[k].astype(F32)
-    scaled = (stream * gain_ref[:, pl.ds(start, WIN)]).astype(BF16)
+    by_parity(lax.rem(dp, 2), lambda skip: arrived(wo_blocks(15, skip, HALF), a2a_r.at[0]))
+    project(0)
 
     def either(c, f):
         zero, one = f(0), f(1)
@@ -364,16 +382,26 @@
         there = block(j, 2, core, i)
         return remote(there, there, sib_s, sib_r, sibling)
 
-    for j in range(4):
-        x_v[j, core, place(j, 2, core), place(j, 1, core), place(j, 0, core)] = scaled[
-            :, 128 * j : 128 * j + 128
-        ]
-    for j in (1, 2, 3, 0):
-        spread(j)
-
+    arrived(res_recv.at[pl.ds(0, 15)], rb_r)
+    res = jnp.concatenate([res_recv[k] for k in range(16)], axis=0)
     st_send[...] = jnp.zeros_like(st_send)
-    for j in range(4):
-        st_send[pl.ds(j, 16, stride=8), :] = stream[:, 128 * j : 128 * j + 128]
+
+    def send_half(half):
+        arrived(rs_recv.at[half, pl.ds(0, 7)], rs_r.at[half])
+        stream = res[:, half * HALF : half * HALF + HALF]
+        for k in range(8):
+            stream = stream + rs_recv[half, k].astype(F32)
+        scaled = (stream * gain_ref[:, pl.ds(start + half * HALF, HALF)]).astype(BF16)
+        for j in (1, 0):
+            at = place(2 * half + j, 2, core), place(2 * half + j, 1, core), place(2 * half + j, 0, core)
+            x_v[(2 * half + j, core, *at)] = scaled[:, 128 * j : 128 * j + 128]
+            spread(2 * half + j)
+        for j in range(2):
+            st_send[pl.ds(2 * half + j, 16, stride=8), :] = stream[:, 128 * j : 128 * j + 128]
+
+    send_half(1)
+    send_half(0)
+
     st_recv[dp] = st_send[pl.ds(pl.multiple_of(dp * 8, 8), 8), :]
 
     def st_copy(n):
@@ -382,28 +410,31 @@
             st_send.at[pl.ds(there, 8)], st_recv.at[dp], st_s, st_r, at_dp(PLANE[n])
         )
 
-    for back in (0, 1, 3, 2):
-        for j in (1, 2, 3, 0):
-            rows_on(j, back)
-    for j in (1, 2, 3, 0):
-        to_sibling(j, 0).start()
+    for tiles in ((3, 2), (1, 0)):
+        for back in (0, 1, 3, 2):
+            for j in tiles:
+                rows_on(j, back)
+        for j in tiles:
+            to_sibling(j, 0).start()
 
     for n in range(15):
         st_copy(n).start()
 
     def wo_sent(skip):
         for n, other in ((7, skip), (8, 128 - skip)):
-            sent(wo_blocks(n, other), a2a_s.at[other // 128])
+            sent(wo_blocks(n, other, HALF), a2a_s.at[other // 128])
 
     by_parity(lax.rem(dp, 2), wo_sent)
+    sent(wo_blocks(15, HALF, WIN), a2a_s.at[2])
     sent(res_recv.at[pl.ds(0, 15)], rb_s)
     sent(vals_all.at[0, pl.ds(0, 3)], val_s.at[0])
     sent(vals_all.at[pl.ds(0, 3)], val_s.at[1])
     sent(lat_recv.at[pl.ds(0, 7)], lat_s)
-    sent(rs_recv.at[pl.ds(0, 7)], rs_s)
+    for half in range(2):
+        sent(rs_recv.at[half, pl.ds(0, 7)], rs_s.at[half])
 
     for i in (1, 3, 2):
-        for j in (0, 1, 2, 3):
+        for j in (2, 3, 1, 0):
             arrived(x_v.at[0, 0, 0] if j else x_v.at[0, 0, 0, pl.ds(0, 2)], ag_r.at[j * 7 + 3 + i])
             to_sibling(j, i).start()
     arrived(x_v.at[:, 0], sib_r)
@@ -420,35 +451,24 @@
 
     def up_step(k, carry):
         g, u, sq = carry
-        tiles = []
-        for odd in range(2):
-            for j in range(odd, 4):
-                tiles.append(tile_of(j, k // 2, 2 * lax.rem(k, 2) + odd))
+        tiles = [tile_of(j, k, y) for y in range(4) for j in range(y % 2, 4)]
         for n, tile in enumerate(tiles):
             f = tile.astype(F32)
-            sq = sq + f * f * ig2_v[:, pl.ds(pl.multiple_of(k * 896 + n * 128, 128), 128)]
+            sq = sq + f * f * ig2_v[:, pl.ds(pl.multiple_of(k * 1792 + n * 128, 128), 128)]
         x = jnp.concatenate(tiles, axis=1)
-        rows = pl.ds(pl.multiple_of(k * 896, 896), 896)
+        rows = pl.ds(pl.multiple_of(k * 1792, 1792), 1792)
         return g + dot(x, wg_v[rows, :]), u + dot(x, wu_v[rows, :]), sq
 
     zero = jnp.zeros((128, FF), F32)
-    g, u, sq = lax.fori_loop(0, 8, up_step, (zero, zero, jnp.zeros((128, 128), F32)))
+    g, u, sq = lax.fori_loop(
+        0, 4, up_step, (zero, zero, jnp.zeros((128, 128), F32)), unroll=True
+    )
     factor = lax.rsqrt(jnp.sum(sq, axis=1, keepdims=True) * (1.0 / D) + EPS)
     g = g * factor
     act = (g / (1.0 + jnp.exp(-g))) * (u * factor * coef_col)
     act = act.astype(BF16)
 
-    bits = {"c": 6, "z": 4, "x": 2, "y": 0}
-    acts = []
-    for p in range(3):
-
-        def source(r):
-            src = jnp.left_shift(jnp.bitwise_xor(jnp.right_shift(r, 6), core), bits["c"])
-            for a, shift in zip(ORDERS[p], (4, 2, 0)):
-                src = src + jnp.left_shift(jnp.bitwise_and(jnp.right_shift(r, shift), 3), bits[a])
-            return src
-
-        acts.append(dot(onehot(128, source), act).astype(BF16))
+    acts = [dot(order_v[3 + p], act).astype(BF16) for p in range(3)]
 
     def core_copy(s):
         p, at, w = PIECES[s]
@@ -482,11 +502,28 @@
         for i in (2, 1, 3):
             sum1(s, i).start()
 
-    for s in range(len(PIECES) + 2):
-        if s < len(PIECES):
-            down(s)
-        if s >= 2:
-            pair(s - 2)
+    def direct_copy(p, other, i):
+        axis = ORDERS[p][0]
+        target = along(axis, i)
+        return remote(
+            pd.at[p, other, lax.rem(pos[axis] + i, 4)], pdr.at[p, core * 4 + pos[axis]],
+            pd_s, pd_r.at[p], crossed(target) if other else target,
+        )
+
+    def direct(p):
+        first = PARTS[p][0]
+        o = dot(acts[p], wd_v[:, first : first + DIRECT])
+        pd[p] = o.reshape(2, 4, 16, DIRECT).astype(BF16)
+        for other, i in ((1, 2), (0, 2), (1, 1), (1, 3), (0, 1), (0, 3), (1, 0)):
+            direct_copy(p, other, i).start()
+        pdr[p, core * 4 + pos[ORDERS[p][0]]] = pd[p, 0, pos[ORDERS[p][0]]]
+
+    for p in range(3):
+        direct(p)
+    for s in range(3):
+        down(s)
+    for s in range(3):
+        pair(s)
 
     def my_row(p):
         return pos[ORDERS[p][1]] * 4 + pos[ORDERS[p][2]]
@@ -500,10 +537,15 @@
 
     q2f[...] = jnp.zeros_like(q2f)
     for p, (first, w) in enumerate(PARTS):
-        arrived(p1r.at[p, :, :, pl.ds(0, w)], p1_r.at[p])
-        o = p1[p, pos[ORDERS[p][0]], :, 0:w].astype(F32)
+        arrived(pdr.at[p, pl.ds(0, 7)], pd_r.at[p])
+        o = pdr[p, 0].astype(F32)
+        for i in range(1, 8):
+            o = o + pdr[p, i].astype(F32)
+        arrived(p1r.at[p, :, :, pl.ds(DIRECT, w - DIRECT)], p1_r.at[p])
+        rest = p1[p, pos[ORDERS[p][0]], :, DIRECT:w].astype(F32)
         for i in range(3):
-            o = o + p1r[p, i, :, 0:w].astype(F32)
+            rest = rest + p1r[p, i, :, DIRECT:w].astype(F32)
+        o = jnp.concatenate([o, rest], axis=1)
         for j in range(w // 128):
             q2f[pl.ds(j, 16, stride=SPAN), :] = o[:, 128 * j : 128 * j + 128]
         q2[p] = q2f[...].reshape(16, SPAN, 128).astype(BF16)
@@ -526,8 +568,9 @@
     sent(x_v.at[pl.ds(0, 3), 0, pl.ds(0, 3)], ag_s.at[2])
     sent(x_v.at[pl.ds(0, 2), 0, 0, pl.ds(0, 3)], ag_s.at[3])
     sent(x_v.at[:, 0], sib_s)
-    sent(wd_v.at[pl.ds(0, 64)], cs_s)
-    sent(wd_v.at[pl.ds(0, 48)], p1_s)
+    sent(wd_v.at[pl.ds(0, 64), pl.ds(0, D - 3 * DIRECT)], cs_s)
+    sent(wd_v.at[pl.ds(0, 48), pl.ds(0, D - 3 * DIRECT)], p1_s)
+    sent(pdr.at[:, pl.ds(0, 7)], pd_s)
 
     for p, (first, w) in enumerate(PARTS):
         arrived(q2r.at[p, pl.ds(0, 15)], p2_r.at[p])
@@ -573,8 +616,8 @@
             pltpu.VMEM((8, 8, LAT + 128), BF16),
             pltpu.VMEM((8, 1152), BF16),
             pltpu.VMEM((4, 4, 8, 1152), BF16),
-            pltpu.VMEM((8, 16, WIN), BF16),
-            pltpu.VMEM((8, 16, WIN), BF16),
+            pltpu.VMEM((2, 8, 16, HALF), BF16),
+            pltpu.VMEM((2, 8, 16, HALF), BF16),
             pltpu.VMEM((128, 128), F32),
             pltpu.VMEM((16, 8, 128), F32),
             pltpu.VMEM((4, 2, 4, 4, 4, 16, 128), BF16),
@@ -588,10 +631,13 @@
             pltpu.VMEM((3, 16, SPAN, 128), BF16),
             pltpu.VMEM((3, 16, SPAN, 128), BF16),
             pltpu.VMEM((D // 128, 128), F32),
+            pltpu.VMEM((6, 128, 128), BF16),
+            pltpu.VMEM((3, 2, 4, 16, DIRECT), BF16),
+            pltpu.VMEM((3, 8, 16, DIRECT), BF16),
             dma((NCHUNK + 11,)),
-            dma((2,)), dma, dma, dma, dma, dma, dma((2,)), dma((2,)),
-            dma, dma, dma, dma, dma((4,)), dma((28,)), dma, dma,
-            dma, dma((6,)), dma, dma((3,)), dma, dma((3,)),
+            dma((3,)), dma((2,)), dma, dma, dma, dma, dma((2,)), dma((2,)),
+            dma((2,)), dma((2,)), dma, dma, dma((4,)), dma((28,)), dma, dma,
+            dma, dma((3,)), dma, dma((3,)), dma, dma((3,)), dma, dma((3,)),
         ],
         compiler_params=pltpu.CompilerParams(
             collective_id=0, has_side_effects=True, vmem_limit_bytes=56 * 1024 * 1024

time: 60.8 us -> 57.7 us (0.949)
  Pallas kernels: 58.2 us -> 55.5 us
    pallas_call x1, Pallas kernels: 58.2 us -> 55.5 us  [on_device(): pl.pallas_call(layer, out_shape=jax.ShapeDtypeStruct((D // 128, 128), BF1...]
where the time goes in v4:
time: 57.7 us; the launch traced here: 57.5 us
  Pallas kernels  55.5 us (96%)
  local copies, waits for them, and re-layouts  1.34 us (2%)
  between operations  0.66 us (1%)
    pallas_call x1, Pallas kernels, on_device(): pl.pallas_call(layer, out_shape=jax.ShapeDtypeStruct((D // 128, 128), BF1...  55.5 us
    unnamed x1, local copies, waits for them, and re-layouts  1.34 us

profile of v4, /device:TPU:0, one launch (start us, length us, event | category | flops | bytes accessed | tf_op | source)
XLA Modules:
  0.0 57.5 jit_solution(847968886895695049)
XLA Ops:
  0.7 55.5 %shard_map.118 = bf16[56,128]{1,0:T(8,128)(2,1)} custom-call(s32[1]{0:T(128)S(6)} %copy.16.len_hbm, s32[1,8]{1,0:T(1,128)} %ids_hbm.1, f32[1,8]{1,0:T(1,128)} %rw_hbm.1, bf16[1,7168]{1,0:T(2,128)(2,1)} %res_hbm.1, bf16[1,64,576]{2,1,0:T(8,128)(2,1)} %q_hbm.1, f32[1,7168]{1,0:T(1,128)} %bitcast.15, bf16[1,576,4096]{2,1,0:T(8,128)(2,1)} %bitcast.10, ...), custom_call_target="tpu_custom_call" | custom-call | tf_op jit(solution)/shard_map/pallas_call | solution.py:594
  56.2 1.3 %copy.15 = bf16[1,1,56,128]{3,1,2,0:T(2,128)(2,1)} copy(bf16[1,1,56,128]{3,2,1,0:T(8,128)(2,1)} %bitcast.14) | data formatting | bytes 28672

commit v5 on v4

--- a/solution.py
+++ b/solution.py
@@ -104,15 +104,6 @@
     def arrived(ref, sem):
         remote(ref, ref, sem, sem, sibling).wait_recv()
 
-    barrier = pltpu.get_barrier_semaphore()
-    peers = [at_dp(step) for step in PLANE] + [at_t(step) for step in LINE]
-    for d in (1, 2, 3):
-        for e in (1, 2, 3):
-            peers += [in_plane("x", "z", (d, e)), in_plane("y", "z", (d, e))]
-        peers += [crossed(along("x", d)), crossed(along("y", d))]
-    for peer in peers:
-        pl.semaphore_signal(barrier, inc=1, device_id=peer, device_id_type=MESH)
-
     def cache_copy(i):
         return pltpu.make_async_copy(
             cache_hbm.at[0, :, pl.ds(pl.multiple_of(i * CHUNK, CHUNK), CHUNK)],
@@ -135,6 +126,15 @@
         cache_copy(i).start()
     for copy in small[3:]:
         copy.start()
+    barrier = pltpu.get_barrier_semaphore()
+    peers = [at_dp(step) for step in PLANE] + [at_t(step) for step in LINE]
+    for d in (1, 2, 3):
+        for e in (1, 2, 3):
+            peers += [in_plane("x", "z", (d, e)), in_plane("y", "z", (d, e))]
+        peers += [crossed(along("x", d)), crossed(along("y", d))]
+    for peer in peers:
+        pl.semaphore_signal(barrier, inc=1, device_id=peer, device_id_type=MESH)
+
     start = pl.multiple_of(window_start(dp), 128)
     own_wo = local(6, wo_hbm.at[:, :, pl.ds(start, WIN)], wo_recv.at[:, dp])
     own_wo.start()

time: 57.7 us -> 57.5 us (level)
  no operation moved by 1% of the time
where the time goes in v5:
time: 57.5 us; the launch traced here: 57.3 us
  Pallas kernels  55.3 us (96%)
  local copies, waits for them, and re-layouts  1.34 us (2%)
  between operations  0.66 us (1%)
    pallas_call x1, Pallas kernels, on_device(): pl.pallas_call(layer, out_shape=jax.ShapeDtypeStruct((D // 128, 128), BF1...  55.3 us
    unnamed x1, local copies, waits for them, and re-layouts  1.34 us

profile of v5, /device:TPU:0, one launch (start us, length us, event | category | flops | bytes accessed | tf_op | source)
XLA Modules:
  0.0 57.3 jit_solution(2597288736903005827)
XLA Ops:
  0.7 55.3 %shard_map.118 = bf16[56,128]{1,0:T(8,128)(2,1)} custom-call(s32[1]{0:T(128)S(6)} %copy.16.len_hbm, s32[1,8]{1,0:T(1,128)} %ids_hbm.1, f32[1,8]{1,0:T(1,128)} %rw_hbm.1, bf16[1,7168]{1,0:T(2,128)(2,1)} %res_hbm.1, bf16[1,64,576]{2,1,0:T(8,128)(2,1)} %q_hbm.1, f32[1,7168]{1,0:T(1,128)} %bitcast.15, bf16[1,576,4096]{2,1,0:T(8,128)(2,1)} %bitcast.10, ...), custom_call_target="tpu_custom_call" | custom-call | tf_op jit(solution)/shard_map/pallas_call | solution.py:594
  56.0 1.3 %copy.15 = bf16[1,1,56,128]{3,1,2,0:T(2,128)(2,1)} copy(bf16[1,1,56,128]{3,2,1,0:T(8,128)(2,1)} %bitcast.14) | data formatting | bytes 28672

commit v6 on v5

--- a/solution.py
+++ b/solution.py
@@ -354,7 +354,7 @@
                     for name in ("dp", "tensor")
                 }
                 remote(
-                    here, here, ag_s.at[0 if j else 1], ag_r.at[j * 7 + step[1]], target
+                    here, here, ag_s.at[0 if j else 1], ag_r.at[j * 4 + step[1]], target
                 ).start()
 
         if j == 0:
@@ -365,12 +365,12 @@
     def rows_on(j, back):
         def go():
             n = 4 if back else 3
-            arrived(x_v.at[0, 0, 0, 0, pl.ds(0, n)], ag_r.at[j * 7 + back])
+            arrived(x_v.at[0, 0, 0, 0, pl.ds(0, n)], ag_r.at[j * 4 + back])
             row = lax.rem(place(j, 1, core) - back + 4, 4)
             here = x_v.at[j, core, place(j, 2, core), row]
             for i in (2, 1, 3):
                 remote(
-                    here, here, ag_s.at[3 if j == 0 else 2], ag_r.at[j * 7 + 3 + i], partner(j, 2, i)
+                    here, here, ag_s.at[3 if j == 0 else 2], ag_r.at[16 + (j // 2) * 3 + i - 1], partner(j, 2, i)
                 ).start()
 
         if j == 0:
@@ -434,9 +434,10 @@
         sent(rs_recv.at[half, pl.ds(0, 7)], rs_s.at[half])
 
     for i in (1, 3, 2):
-        for j in (2, 3, 1, 0):
-            arrived(x_v.at[0, 0, 0] if j else x_v.at[0, 0, 0, pl.ds(0, 2)], ag_r.at[j * 7 + 3 + i])
-            to_sibling(j, i).start()
+        for half, both in ((1, x_v.at[pl.ds(0, 2), 0, 0]), (0, x_v.at[pl.ds(0, 3), 0, 0, pl.ds(0, 2)])):
+            arrived(both, ag_r.at[16 + half * 3 + i - 1])
+            for j in (2 * half + 1, 2 * half):
+                to_sibling(j, i).start()
     arrived(x_v.at[:, 0], sib_r)
     for copy in w_copies:
         copy.wait()
@@ -636,7 +637,7 @@
             pltpu.VMEM((3, 8, 16, DIRECT), BF16),
             dma((NCHUNK + 11,)),
             dma((3,)), dma((2,)), dma, dma, dma, dma, dma((2,)), dma((2,)),
-            dma((2,)), dma((2,)), dma, dma, dma((4,)), dma((28,)), dma, dma,
+            dma((2,)), dma((2,)), dma, dma, dma((4,)), dma((22,)), dma, dma,
             dma, dma((3,)), dma, dma((3,)), dma, dma((3,)), dma, dma((3,)),
         ],
         compiler_params=pltpu.CompilerParams(

time: 57.5 us -> 57.4 us (level)
  no operation moved by 1% of the time
where the time goes in v6:
time: 57.4 us; the launch traced here: 57.3 us
  Pallas kernels  55.3 us (96%)
  local copies, waits for them, and re-layouts  1.34 us (2%)
  between operations  0.66 us (1%)
    pallas_call x1, Pallas kernels, on_device(): pl.pallas_call(layer, out_shape=jax.ShapeDtypeStruct((D // 128, 128), BF1...  55.3 us
    unnamed x1, local copies, waits for them, and re-layouts  1.34 us

profile of v6, /device:TPU:0, one launch (start us, length us, event | category | flops | bytes accessed | tf_op | source)
XLA Modules:
  0.0 57.3 jit_solution(16264722339833731797)
XLA Ops:
  0.7 55.3 %shard_map.118 = bf16[56,128]{1,0:T(8,128)(2,1)} custom-call(s32[1]{0:T(128)S(6)} %copy.16.len_hbm, s32[1,8]{1,0:T(1,128)} %ids_hbm.1, f32[1,8]{1,0:T(1,128)} %rw_hbm.1, bf16[1,7168]{1,0:T(2,128)(2,1)} %res_hbm.1, bf16[1,64,576]{2,1,0:T(8,128)(2,1)} %q_hbm.1, f32[1,7168]{1,0:T(1,128)} %bitcast.15, bf16[1,576,4096]{2,1,0:T(8,128)(2,1)} %bitcast.10, ...), custom_call_target="tpu_custom_call" | custom-call | tf_op jit(solution)/shard_map/pallas_call | solution.py:595
  55.9 1.3 %copy.15 = bf16[1,1,56,128]{3,1,2,0:T(2,128)(2,1)} copy(bf16[1,1,56,128]{3,2,1,0:T(8,128)(2,1)} %bitcast.14) | data formatting | bytes 28672
